TPU v7x, 128 devices: a whole 4x4x4 slice. The times are simulated.
128 devices in a mesh: grp: 8 (over x_hi, y), tp: 16 (over x_lo, z, core).
Axes of the slice: x: 4 (x_hi: 2, x_lo: 2; x = x_hi * 2 + x_lo), y: 4, z: 4, core: 2. Of those that a mesh axis runs over, the one named last changes fastest.
Arguments:
- tokens: bfloat16 [16384, 2560], P(('grp', 'tp')), may hold values from -6 to 6
- grad_out: bfloat16 [16384, 2560], P(('grp', 'tp')), may hold values from -6 to 6
- route_score: float32 [16384], P(('grp', 'tp')), may hold values from 0.2 to 1
- expert_ids: int32 [16384], P(('grp', 'tp')), may hold values from 0 to 127, as said below
- slots: int32 [16384], P(('grp', 'tp')), may hold values from 0 to 5, as said below
- counts: int32 [128, 8], P(('grp', 'tp')), may hold values from 0 to 4, as said below
- shared_gate_pre: bfloat16 [16384, 4096], P('grp', 'tp'), may hold values from -6 to 6
- shared_up_pre: bfloat16 [16384, 4096], P('grp', 'tp'), may hold values from -6 to 6
- shared_w_gate: bfloat16 [2560, 4096], P(None, 'tp'), may hold values from -0.125 to 0.125
- shared_w_up: bfloat16 [2560, 4096], P(None, 'tp'), may hold values from -0.125 to 0.125
- shared_w_down: bfloat16 [4096, 2560], P('tp'), may hold values from -0.09375 to 0.09375
- w_gate: bfloat16 [8, 2560, 4096], P('grp', None, 'tp'), may hold values from -0.125 to 0.125
- w_up: bfloat16 [8, 2560, 4096], P('grp', None, 'tp'), may hold values from -0.125 to 0.125
- w_down: bfloat16 [8, 4096, 2560], P('grp', 'tp'), may hold values from -0.09375 to 0.09375
Outputs:
- grad_tokens: bfloat16 [16384, 2560], P(('grp', 'tp'))
- grad_score: float32 [16384], P(('grp', 'tp'))
- grad_shared_gate: bfloat16 [2560, 4096], P('grp', 'tp')
- grad_shared_up: bfloat16 [2560, 4096], P('grp', 'tp')
- grad_shared_down: bfloat16 [4096, 2560], P('tp', 'grp')
- grad_gate: bfloat16 [8, 2560, 4096], P('grp', None, 'tp')
- grad_up: bfloat16 [8, 2560, 4096], P('grp', None, 'tp')
- grad_down: bfloat16 [8, 4096, 2560], P('grp', 'tp')
Inputs may be any that keep to these rules, and one draw needn't show every extreme that they name: `expert_ids`: ids below 8 name the experts of this window; the others name experts outside it. A device routes at most 6 tokens to one expert of the window. `slots`: on one device, the tokens of one expert of the window hold the numbers 0 to n - 1, each once, where n is at least that expert's count; only those below the count are live. `counts`: at most the number of the device's tokens routed to that expert; in every draw some device has exactly 4 live rows for each expert of the window.
All inputs are finite; a program needn't handle non-finite values.
Results may differ from a plain program's by a relative error of at most 0.022.
Values may be sent and summed in bfloat16 or wider, within the bound.
A program may use at most 192 MiB of HBM per device.

v0:
```python
import jax
import jax.numpy as jnp
from jax import lax
from jax.sharding import PartitionSpec as P

CAP = 4


def swish_parts(gate_pre, up_pre, hidden_grad):
    sigma = jax.nn.sigmoid(gate_pre)
    swish = gate_pre * sigma
    slope = sigma * (1.0 + gate_pre * (1.0 - sigma))
    return (
        (hidden_grad * up_pre * slope).astype(jnp.bfloat16),
        (hidden_grad * swish).astype(jnp.bfloat16),
    )


def contract_rows(left, right):
    return lax.dot_general(
        left, right, (((0,), (0,)), ((), ())), preferred_element_type=jnp.float32
    )


def contract_cols(left, right):
    return lax.dot_general(
        left, right, (((1,), (1,)), ((), ())), preferred_element_type=jnp.float32
    )


def shards(
    tokens,
    grad_out,
    route_score,
    expert_ids,
    slots,
    counts,
    shared_gate_pre,
    shared_up_pre,
    shared_w_gate,
    shared_w_up,
    shared_w_down,
    w_gate,
    w_up,
    w_down,
):
    tok_dev, width = tokens.shape
    experts = counts.shape[1]
    members = lax.axis_size("tp")
    sources = lax.axis_size("grp") * members
    tok_group, grad_group = (
        lax.all_gather(tokens, "tp", axis=0, tiled=True),
        lax.all_gather(grad_out, "tp", axis=0, tiled=True),
    )
    gate_f = shared_gate_pre.astype(jnp.float32)
    up_f = shared_up_pre.astype(jnp.float32)
    shared_hidden = (jax.nn.silu(gate_f) * up_f).astype(jnp.bfloat16)
    shared_hgrad = contract_cols(grad_group, shared_w_down)
    shared_dgate, shared_dup = swish_parts(gate_f, up_f, shared_hgrad)
    part_gate = contract_rows(tok_group, shared_dgate)
    part_up = contract_rows(tok_group, shared_dup)
    part_down = contract_rows(shared_hidden, grad_group)
    sum_gate, sum_up, sum_down = (
        lax.psum_scatter(
            part_gate.astype(jnp.bfloat16), "grp", scatter_dimension=0, tiled=True
        ).astype(jnp.float32),
        lax.psum_scatter(
            part_up.astype(jnp.bfloat16), "grp", scatter_dimension=0, tiled=True
        ).astype(jnp.float32),
        lax.psum_scatter(
            part_down.astype(jnp.bfloat16), "grp", scatter_dimension=1, tiled=True
        ).astype(jnp.float32),
    )
    shared_grad_in = lax.psum_scatter(
        (
            contract_cols(shared_dgate, shared_w_gate) + contract_cols(shared_dup, shared_w_up)
        ).astype(jnp.bfloat16),
        "tp",
        scatter_dimension=0,
        tiled=True,
    ).astype(jnp.float32)
    expert_iota = jnp.arange(experts, dtype=jnp.int32)
    match = expert_ids[:, None] == expert_iota[None, :]
    own_count = jnp.sum(jnp.where(match, counts, 0), axis=1)
    live = (expert_ids < experts) & (slots < own_count)
    position = expert_ids * CAP + slots
    row_iota = jnp.arange(experts * CAP, dtype=jnp.int32)
    select = ((row_iota[:, None] == position[None, :]) & live[None, :]).astype(jnp.bfloat16)
    scaled = (route_score[:, None] * tokens.astype(jnp.float32)).astype(jnp.bfloat16)
    send_in = (
        jnp.dot(select, scaled, preferred_element_type=jnp.float32)
        .astype(jnp.bfloat16)
        .reshape(experts, CAP, width)
    )
    send_grad = (
        jnp.dot(select, grad_out, preferred_element_type=jnp.float32)
        .astype(jnp.bfloat16)
        .reshape(experts, CAP, width)
    )
    wide_in = jnp.broadcast_to(send_in[:, None], (experts, members, CAP, width)).reshape(
        sources, CAP, width
    )
    wide_grad = jnp.broadcast_to(send_grad[:, None], (experts, members, CAP, width)).reshape(
        sources, CAP, width
    )
    rows_in, rows_grad = (
        lax.all_to_all(wide_in, ("grp", "tp"), split_axis=0, concat_axis=0, tiled=True),
        lax.all_to_all(wide_grad, ("grp", "tp"), split_axis=0, concat_axis=0, tiled=True),
    )
    routed_in = rows_in.reshape(sources * CAP, width)
    routed_grad = rows_grad.reshape(sources * CAP, width)
    gate = jnp.dot(routed_in, w_gate[0], preferred_element_type=jnp.float32)
    up = jnp.dot(routed_in, w_up[0], preferred_element_type=jnp.float32)
    hidden = (jax.nn.silu(gate) * up).astype(jnp.bfloat16)
    hgrad = contract_cols(routed_grad, w_down[0])
    dgate, dup = swish_parts(gate, up, hgrad)
    grad_down = contract_rows(hidden, routed_grad).astype(jnp.bfloat16)[None]
    grad_gate = contract_rows(routed_in, dgate).astype(jnp.bfloat16)[None]
    grad_up = contract_rows(routed_in, dup).astype(jnp.bfloat16)[None]
    partial_value = contract_cols(dgate, w_gate[0]) + contract_cols(dup, w_up[0])
    pieces = lax.all_to_all(
        partial_value.astype(jnp.bfloat16).reshape(sources, CAP, width),
        ("grp", "tp"),
        split_axis=0,
        concat_axis=0,
        tiled=True,
    )
    routed_back = jnp.sum(
        pieces.astype(jnp.float32).reshape(experts, members, CAP, width), axis=1
    ).astype(jnp.bfloat16)
    combined = contract_rows(select, routed_back.reshape(experts * CAP, width))
    grad_score = jnp.sum(tokens.astype(jnp.float32) * combined, axis=1)
    grad_tokens = (shared_grad_in + route_score[:, None] * combined).astype(jnp.bfloat16)
    return (
        grad_tokens,
        grad_score,
        sum_gate.astype(jnp.bfloat16),
        sum_up.astype(jnp.bfloat16),
        sum_down.astype(jnp.bfloat16),
        grad_gate,
        grad_up,
        grad_down,
    )


def solution(mesh):
    placed = (
        P(("grp", "tp"), None),
        P(("grp", "tp"), None),
        P(("grp", "tp")),
        P(("grp", "tp")),
        P(("grp", "tp")),
        P(("grp", "tp"), None),
        P("grp", "tp"),
        P("grp", "tp"),
        P(None, "tp"),
        P(None, "tp"),
        P("tp", None),
        P("grp", None, "tp"),
        P("grp", None, "tp"),
        P("grp", "tp", None),
    )
    return jax.shard_map(
        shards,
        mesh=mesh,
        in_specs=placed,
        out_specs=(
            P(("grp", "tp"), None),
            P(("grp", "tp")),
            P("grp", "tp"),
            P("grp", "tp"),
            P("tp", "grp"),
            P("grp", None, "tp"),
            P("grp", None, "tp"),
            P("grp", "tp", None),
        ),
        check_vma=False,
    )
```

profile of v0, /device:TPU:6, one launch (start us, length us, event | category | flops | bytes accessed | tf_op | source)
XLA Modules:
  0.0 535.8 jit_solution(4065418339350491594)
XLA Ops:
  7.2 0.0 copy-start
  7.2 0.0 all-gather.3.cloned.1.call-start
  7.2 0.7 all-gather.3.cloned.1.call-update
  7.9 0.0 all-gather.5.cloned.1.call-start
  8.0 0.7 all-gather.5.cloned.1.call-update
  8.7 0.0 reduce-scatter.9.cloned.1.call-start
  8.7 65.3 %all-gather.3.cloned.1.call-done = bf16[2048,2560]{1,0:T(8,128)(2,1)} async-done(((bf16[128,2560]{1,0:T(8,128)(2,1)}), bf16[2048,2560]{1,0:T(8,128)(2,1)}) %all-gather.3.cloned.1.call-update) | async-done | bytes 10485776 | tf_op jit(solution)/shard_map/all_gather | solution.py:53
  74.0 8.5 %fusion.6 = (bf16[2048,256]{1,0:T(8,128)(2,1)S(1)}, f32[2048,256]{1,0:T(8,128)S(1)}) fusion(bf16[2048,256]{1,0:T(8,128)(2,1)} %param.21, bf16[2048,256]{1,0:T(8,128)(2,1)} %param.20, bf16[2048,2560]{1,0:T(8,128)(2,1)} %all-gather.3.cloned.1.call-done, bf16[256,2560]{1,0:T(8,128)(2,1)} %param.24), kind=kOutput, calls=%fused_computation.22 | convolution fusion | flops 2690646016 | bytes 17039360 | tf_op jit(solution)/shard_map/dot_general | solution.py:26
  82.5 0.0 copy-start.4
  82.5 9.0 %fusion.42 = f32[2048,2560]{1,0:T(8,128)} fusion(bf16[2048,256]{1,0:T(8,128)(2,1)S(1)} %get-tuple-element.36, bf16[2560,256]{1,0:T(8,128)(2,1)S(1)} %copy-done), kind=kOutput, calls=%fused_computation.65 | convolution fusion | flops 2684354560 | bytes 23330816 | tf_op jit(solution)/shard_map/dot_general | solution.py:26
  91.6 15.2 %add_convert_fusion = bf16[2048,2560]{1,0:T(8,128)(2,1)} fusion(f32[2048,2560]{1,0:T(8,128)} %fusion.42, bf16[2560,256]{1,0:T(8,128)(2,1)} %param.23, f32[2048,256]{1,0:T(8,128)S(1)} %get-tuple-element.37, bf16[2048,256]{1,0:T(8,128)(2,1)} %param.20), kind=kOutput, calls=%fused_computation | convolution fusion | flops 2698510336 | bytes 35913728 | tf_op jit(solution)/shard_map/dot_general | solution.py:26
  106.8 0.0 reduce-scatter.9.cloned.1.call-update
  106.8 0.6 copy-done.25
  107.4 0.0 copy-done.27
  107.4 0.1 select_reduce_fusion
  107.5 0.4 copy-done.11
  107.9 0.2 convolution_convert_fusion.7
  108.1 0.1 broadcast_in_dim.47
  108.2 2.2 broadcast_in_dim.48
  110.3 9.6 %all-to-all-start = ((bf16[128,4,2560]{2,1,0:T(4,128)(2,1)}), bf16[128,4,2560]{2,1,0:T(4,128)(2,1)}, u32[]{:S(2)}, u32[]{:S(2)}) async-start(bf16[128,4,2560]{2,1,0:T(4,128)(2,1)} %bitcast.54), calls=%async_computation.1 | async-start | bytes 5242880 | tf_op jit(solution)/shard_map/all_to_all | solution.py:108
  120.0 0.3 convolution_convert_fusion.6
  120.3 0.1 broadcast_in_dim.49
  120.4 43.7 %all-to-all-done = bf16[128,4,2560]{2,1,0:T(4,128)(2,1)} async-done(((bf16[128,4,2560]{2,1,0:T(4,128)(2,1)}), bf16[128,4,2560]{2,1,0:T(4,128)(2,1)}, u32[]{:S(2)}, u32[]{:S(2)}) %all-to-all-start) | async-done | bytes 2621472 | tf_op jit(solution)/shard_map/all_to_all | solution.py:108
  164.1 2.2 broadcast_in_dim.50
  166.4 6.9 %all-to-all-start.1 = ((bf16[128,4,2560]{2,1,0:T(4,128)(2,1)}), bf16[128,4,2560]{2,1,0:T(4,128)(2,1)}, u32[]{:S(2)}, u32[]{:S(2)}) async-start(bf16[128,4,2560]{2,1,0:T(4,128)(2,1)} %bitcast.53), calls=%async_computation.2 | async-start | bytes 5242880 | tf_op jit(solution)/shard_map/all_to_all | solution.py:107
  173.3 0.2 reduce-scatter.11.cloned.1.call-start
  173.5 9.9 %convolution_convert_fusion.3 = bf16[256,2560]{0,1:T(8,128)(2,1)} fusion(bf16[2048,2560]{1,0:T(8,128)(2,1)} %all-gather.3.cloned.1.call-done, bf16[2048,256]{1,0:T(8,128)(2,1)} %param.21, bf16[2048,256]{1,0:T(8,128)(2,1)S(1)} %copy-done.8), kind=kOutput, calls=%fused_computation.5 | convolution fusion | flops 2689204224 | bytes 13893632 | tf_op jit(solution)/shard_map/dot_general | solution.py:20
  183.4 0.0 reduce-scatter.11.cloned.1.call-update
  183.5 0.0 reduce-scatter.13.cloned.1.call-start
  183.5 5.3 reshape.47
  188.8 33.7 %all-to-all-done.1 = bf16[128,4,2560]{2,1,0:T(4,128)(2,1)} async-done(((bf16[128,4,2560]{2,1,0:T(4,128)(2,1)}), bf16[128,4,2560]{2,1,0:T(4,128)(2,1)}, u32[]{:S(2)}, u32[]{:S(2)}) %all-to-all-start.1) | async-done | bytes 2621472 | tf_op jit(solution)/shard_map/all_to_all | solution.py:107
  222.5 5.4 %reshape.49 = bf16[512,2560]{1,0:T(8,128)(2,1)} reshape(bf16[128,4,2560]{2,1,0:T(4,128)(2,1)} %all-to-all-done.1) | data formatting | bytes 5242880 | tf_op jit(solution)/shard_map/reshape | solution.py:110
  227.9 3.9 fusion.17
  231.8 8.1 %fusion = bf16[2560,256]{0,1:T(8,128)(2,1)} fusion(bf16[2048,256]{1,0:T(8,128)(2,1)S(1)} %copy-done.5, bf16[2048,2560]{1,0:T(8,128)(2,1)} %all-gather.5.cloned.1.call-done), kind=kOutput, calls=%fused_computation.8 | convolution fusion | flops 2685009920 | bytes 12845056 | tf_op jit(solution)/shard_map/dot_general | solution.py:20
  239.9 2.6 copy.28
  242.5 0.0 reduce-scatter.13.cloned.1.call-update
  242.6 0.0 copy-start.17
  242.6 0.0 copy-start.26
  242.6 2.8 fusion.20
  245.4 0.3 copy-done.26
  245.7 0.9 multiply_convert_fusion.2
  246.7 0.0 copy-start.15
  246.7 0.0 copy-start.21
  246.7 0.6 copy-done.12
  247.3 0.9 fusion.15
  248.2 0.4 copy-done.14
  248.6 2.5 add_convert_fusion.1
  251.0 5.6 %reshape.50 = bf16[128,4,2560]{2,1,0:T(4,128)(2,1)} reshape(bf16[512,2560]{1,0:T(8,128)(2,1)} %add_convert_fusion.1) | data formatting | bytes 5242880 | tf_op jit(solution)/shard_map/reshape | solution.py:122
  256.7 7.1 %all-to-all-start.2 = ((bf16[128,4,2560]{2,1,0:T(4,128)(2,1)}), bf16[128,4,2560]{2,1,0:T(4,128)(2,1)}, u32[]{:S(2)}, u32[]{:S(2)}) async-start(bf16[128,4,2560]{2,1,0:T(4,128)(2,1)} %reshape.50), calls=%async_computation.3 | async-start | bytes 5242880 | tf_op jit(solution)/shard_map/all_to_all | solution.py:121
  263.8 0.3 reduce-scatter.15.cloned.1.call-start
  264.1 8.1 %fusion.1 = bf16[2560,256]{0,1:T(8,128)(2,1)} fusion(bf16[2048,2560]{1,0:T(8,128)(2,1)} %all-gather.5.cloned.1.call-done, f32[2048,256]{1,0:T(8,128)S(1)} %get-tuple-element.37, bf16[2048,256]{1,0:T(8,128)(2,1)S(1)} %copy-done.9), kind=kOutput, calls=%fused_computation.9 | convolution fusion | flops 2688679936 | bytes 14942208 | tf_op jit(solution)/shard_map/dot_general | solution.py:20
  272.2 2.5 copy.30
  274.7 0.0 reduce-scatter.15.cloned.1.call-update
  274.7 3.9 fusion.3
  278.6 2.0 fusion.2
  280.6 0.5 copy-done.20
  281.1 2.0 fusion.4
  283.1 21.1 %all-to-all-done.2 = bf16[128,4,2560]{2,1,0:T(4,128)(2,1)} async-done(((bf16[128,4,2560]{2,1,0:T(4,128)(2,1)}), bf16[128,4,2560]{2,1,0:T(4,128)(2,1)}, u32[]{:S(2)}, u32[]{:S(2)}) %all-to-all-start.2) | async-done | bytes 2621472 | tf_op jit(solution)/shard_map/all_to_all | solution.py:121
  304.2 2.9 bitcast_reduce_fusion
  307.1 0.0 reduce-scatter.9.cloned.1.call-done
  307.2 3.0 fusion.14
  310.2 66.2 %reduce-scatter.11.cloned.1.call-done = bf16[256,320]{0,1:T(8,128)(2,1)} async-done(((bf16[256,2560]{0,1:T(8,128)(2,1)}), bf16[256,320]{0,1:T(8,128)(2,1)}) %reduce-scatter.11.cloned.1.call-update) | async-done | bytes 163856 | tf_op jit(solution)/shard_map/reduce_scatter | solution.py:70
  376.4 76.3 %reduce-scatter.13.cloned.1.call-done = bf16[320,256]{1,0:T(8,128)(2,1)} async-done(((bf16[2560,256]{1,0:T(8,128)(2,1)}), bf16[320,256]{1,0:T(8,128)(2,1)}) %reduce-scatter.13.cloned.1.call-update) | async-done | bytes 163856
  452.6 76.3 %reduce-scatter.15.cloned.1.call-done = bf16[320,256]{1,0:T(8,128)(2,1)} async-done(((bf16[2560,256]{1,0:T(8,128)(2,1)}), bf16[320,256]{1,0:T(8,128)(2,1)}) %reduce-scatter.15.cloned.1.call-update) | async-done | bytes 163856
  (47 shorter events, 0.1 us)
Async XLA Ops:
  7.2 75.3 %copy-start = (bf16[2560,256]{1,0:T(8,128)(2,1)S(1)}, bf16[2560,256]{1,0:T(8,128)(2,1)}, u32[]{:S(2)}) copy-start(bf16[2560,256]{1,0:T(8,128)(2,1)} %param.22) | copy-start | bytes 3932164
  7.2 66.8 %all-gather.3.cloned.1.call-start = ((), (), s32[]{:S(2)}) async-start(), calls=%async_computation.7 | async-start | bytes 11141120 | tf_op jit(solution)/shard_map/all_gather | solution.py:53
  7.9 223.9 %all-gather.5.cloned.1.call-start = ((), (), s32[]{:S(2)}) async-start(), calls=%async_computation.9 | async-start | bytes 11141120 | tf_op jit(solution)/shard_map/all_gather | solution.py:52
  8.7 298.5 %reduce-scatter.9.cloned.1.call-start = ((), (), s32[]{:S(2)}) async-start(), calls=%async_computation.8 | async-start | bytes 11141120 | tf_op jit(solution)/shard_map/reduce_scatter | solution.py:74
  82.5 9.1 %copy-start.4 = (bf16[2048,256]{1,0:T(8,128)(2,1)}, bf16[2048,256]{1,0:T(8,128)(2,1)S(1)}, u32[]{:S(2)}) copy-start(bf16[2048,256]{1,0:T(8,128)(2,1)S(1)} %get-tuple-element.36) | copy-start | bytes 3145732
  106.8 0.7 copy-start.25
  106.8 0.7 copy-start.27
  106.8 0.8 copy-start.24
  106.8 1.1 copy-start.11
  110.3 9.6 %copy-start.6 = (bf16[128,2560]{1,0:T(8,128)(2,1)S(1)}, bf16[128,2560]{1,0:T(8,128)(2,1)}, u32[]{:S(2)}) copy-start(bf16[128,2560]{1,0:T(8,128)(2,1)} %param.14) | copy-start | bytes 1966084
  110.3 9.7 %copy-start.23 = (f32[128]{0:T(128)S(1)}, f32[128]{0:T(128)}, u32[]{:S(2)}) copy-start(f32[128]{0:T(128)} %param.16) | copy-start | bytes 1540
  110.3 53.8 %all-to-all-start = ((bf16[128,4,2560]{2,1,0:T(4,128)(2,1)}), bf16[128,4,2560]{2,1,0:T(4,128)(2,1)}, u32[]{:S(2)}, u32[]{:S(2)}) async-start(bf16[128,4,2560]{2,1,0:T(4,128)(2,1)} %bitcast.54), calls=%async_computation.1 | async-start | bytes 5242880 | tf_op jit(solution)/shard_map/all_to_all | solution.py:108
  166.4 7.2 %copy-start.8 = (bf16[2048,256]{1,0:T(8,128)(2,1)S(1)}, bf16[2048,256]{1,0:T(8,128)(2,1)}, u32[]{:S(2)}) copy-start(bf16[2048,256]{1,0:T(8,128)(2,1)} %param.20) | copy-start | bytes 3145732
  166.4 56.1 %all-to-all-start.1 = ((bf16[128,4,2560]{2,1,0:T(4,128)(2,1)}), bf16[128,4,2560]{2,1,0:T(4,128)(2,1)}, u32[]{:S(2)}, u32[]{:S(2)}) async-start(bf16[128,4,2560]{2,1,0:T(4,128)(2,1)} %bitcast.53), calls=%async_computation.2 | async-start | bytes 5242880 | tf_op jit(solution)/shard_map/all_to_all | solution.py:107
  173.3 203.1 %reduce-scatter.11.cloned.1.call-start = ((), (), s32[]{:S(2)}) async-start(), calls=%async_computation.10 | async-start | bytes 1474560 | tf_op jit(solution)/shard_map/reduce_scatter | solution.py:70
  183.5 269.2 %reduce-scatter.13.cloned.1.call-start = ((), (), s32[]{:S(2)}) async-start(), calls=%async_computation.11 | async-start | bytes 1474560
  227.9 3.9 copy-start.5
  239.9 2.6 copy-start.13
  242.5 2.8 copy-start.2
  242.6 2.8 copy-start.17
  242.6 3.2 copy-start.26
  245.7 0.9 copy-start.19
  245.7 1.5 copy-start.12
  246.7 1.5 copy-start.15
  246.7 1.5 copy-start.21
  247.3 1.3 copy-start.14
  256.6 7.4 %copy-start.9 = (bf16[2048,256]{1,0:T(8,128)(2,1)S(1)}, bf16[2048,256]{1,0:T(8,128)(2,1)}, u32[]{:S(2)}) copy-start(bf16[2048,256]{1,0:T(8,128)(2,1)} %param.20) | copy-start | bytes 3145732
  256.7 47.5 %all-to-all-start.2 = ((bf16[128,4,2560]{2,1,0:T(4,128)(2,1)}), bf16[128,4,2560]{2,1,0:T(4,128)(2,1)}, u32[]{:S(2)}, u32[]{:S(2)}) async-start(bf16[128,4,2560]{2,1,0:T(4,128)(2,1)} %reshape.50), calls=%async_computation.3 | async-start | bytes 5242880 | tf_op jit(solution)/shard_map/all_to_all | solution.py:121
  263.8 265.1 %reduce-scatter.15.cloned.1.call-start = ((), (), s32[]{:S(2)}) async-start(), calls=%async_computation.12 | async-start | bytes 1474560
  272.2 2.5 copy-start.22
  274.7 3.9 copy-start.10
  274.7 3.9 copy-start.16
  278.6 2.0 copy-start.3
  278.6 2.0 copy-start.18
  278.6 2.5 copy-start.20
  281.1 247.8 %copy-start.1 = (bf16[2560,256]{1,0:T(8,128)(2,1)S(1)}, bf16[2560,256]{1,0:T(8,128)(2,1)}, u32[]{:S(2)}) copy-start(bf16[2560,256]{1,0:T(8,128)(2,1)} %param.22) | copy-start | bytes 3932164
  283.1 24.1 %copy-start.7 = (bf16[128,2560]{1,0:T(8,128)(2,1)S(1)}, bf16[128,2560]{1,0:T(8,128)(2,1)}, u32[]{:S(2)}) copy-start(bf16[128,2560]{1,0:T(8,128)(2,1)} %param.14) | copy-start | bytes 1966084
Sparse Core Ops, SparseCore 0:
  9.7 64.2 all-gather.2
  75.7 91.0 all-gather.4
  169.3 112.9 reduce-scatter.8
  286.3 89.9 reduce-scatter.10
  380.4 72.1 reduce-scatter.12
  456.7 72.1 reduce-scatter.14
where the time goes:
time: 538 us; the launch traced here: 536 us
  waiting for transfers between devices  384 us (71%)
  matrix products  81.1 us (15%)
  local copies, waits for them, and re-layouts  28.9 us (5%)
  starting transfers between devices  24.3 us (5%)
  between operations  14.4 us (3%)
    unnamed x8, waiting for transfers between devices  154 us
    reduce_scatter x1, waiting for transfers between devices, shards(): lax.psum_scatter(part_down.astype(jnp.bfloat16), 'grp', scatter_dimension...  66.2 us
    all_gather x1, waiting for transfers between devices, shards(): lax.all_gather(grad_out, 'tp', axis=0, tiled=True)  65.3 us
    all_to_all x1, waiting for transfers between devices, shards(): lax.all_to_all(wide_grad, ('grp', 'tp'), split_axis=0, concat_axis=0, til...  43.7 us
    dot_general x6, matrix products, contract_cols(): lax.dot_general(left, right, (((1,), (1,)), ((), ())), preferred_element_...  37 us
    dot_general x7, matrix products, contract_rows(): lax.dot_general(left, right, (((0,), (0,)), ((), ())), preferred_element_...  37 us
    all_to_all x1, waiting for transfers between devices, shards(): lax.all_to_all(wide_in, ('grp', 'tp'), split_axis=0, concat_axis=0, tiled...  33.7 us
    all_to_all x1, waiting for transfers between devices, shards(): lax.all_to_all(partial_value.astype(jnp.bfloat16).reshape(sources, CAP, w...  21.1 us
  transfers between devices with their start and end apart: 9, of which 7 were waited for; matrix products, arithmetic and copies ran while one was open for 21% of the time, Pallas kernels for 0%

commit v1 on v0

v1 whole, which is shorter than its diff:
```python
import functools

import jax
import jax.numpy as jnp
from jax import lax
from jax.experimental import pallas as pl
from jax.experimental.pallas import tpu as pltpu
from jax.sharding import PartitionSpec as P

CAP = 4
MESH = pl.DeviceIdType.MESH
BF, F32 = jnp.bfloat16, jnp.float32
ANY = pl.BlockSpec(memory_space=pl.ANY)
VM = pl.BlockSpec(memory_space=pltpu.VMEM)
SM = pl.BlockSpec(memory_space=pltpu.SMEM)
DIRS = (("+", 1), ("-", -1))


def dot_nn(a, b):
    return lax.dot_general(a, b, (((1,), (0,)), ((), ())), preferred_element_type=F32)


def dot_nt(a, b):
    return lax.dot_general(a, b, (((1,), (1,)), ((), ())), preferred_element_type=F32)


def dot_tn(a, b):
    return lax.dot_general(a, b, (((0,), (0,)), ((), ())), preferred_element_type=F32)


class Place:
    def __init__(self):
        self.g = lax.axis_index("grp")
        self.t = lax.axis_index("tp")
        self.xh, self.y = self.g // 4, self.g % 4
        self.xl, self.z, self.c = self.t // 8, (self.t // 2) % 4, self.t % 2

    def chip(self, dx, dz):
        return ((self.xl + dx) % 2) * 4 + (self.z + dz + 4) % 4

    def member(self, dx, dz, other=False):
        core = 1 - self.c if other else self.c
        return self.chip(dx, dz) * 2 + core

    def at(self, dx, dz, other=False):
        return (self.g, self.member(dx, dz, other))

    def group(self, dh, dy):
        return ((self.xh + dh) % 2) * 4 + (self.y + dy + 4) % 4

    def over(self, dh, dy):
        return (self.group(dh, dy), self.t)


def greet(targets):
    barrier = pltpu.get_barrier_semaphore()
    for target in targets:
        pl.semaphore_signal(barrier, inc=1, device_id=target, device_id_type=MESH)
    pl.semaphore_wait(barrier, len(targets))


def remote(src, dst, ss, rs, target):
    return pltpu.make_async_remote_copy(
        src_ref=src, dst_ref=dst, send_sem=ss, recv_sem=rs, device_id=target, device_id_type=MESH
    )


ARRIVE = {"xB": (1, 0, None, "B"), "xA0": (1, 0, None, "A")}
for _s, _d in DIRS:
    _h = 0 if _d > 0 else 1
    ARRIVE["zA" + _s] = (0, -_d, None, "A")
    ARRIVE["zB" + _s] = (0, -_d, None, "B")
    ARRIVE["zX" + _s] = (1, -_d, None, "B")
    ARRIVE["hA" + _s] = (0, 2, _h, "A")
    ARRIVE["hB" + _s] = (0, 2, _h, "B")
    ARRIVE["hX" + _s] = (1, 2, _h, "B")
    ARRIVE["xA" + _s] = (1, -_d, None, "A")
    ARRIVE["xh" + _s] = (1, 2, _h, "A")
SLOT = {name: i for i, name in enumerate(ARRIVE)}
N_ICI = len(SLOT)
N_SLOT = 2 * N_ICI + 1


class Gather:
    def __init__(self, place, buf, cut, ss, rs):
        self.p, self.buf, self.cut, self.ss, self.rs = place, buf, cut, ss, rs
        self.rows, self.width = buf.shape[1], buf.shape[2]
        self.sent = []

    def ref(self, member, half, part):
        rows = pl.ds(0, self.rows) if half is None else pl.ds(half * (self.rows // 2), self.rows // 2)
        cols = {
            None: pl.ds(0, self.width),
            "A": pl.ds(0, self.cut),
            "B": pl.ds(self.cut, self.width - self.cut),
        }[part]
        return self.buf.at[member, rows, cols]

    def send(self, slot, member, half, part, target):
        ref = self.ref(member, half, part)
        copy = remote(ref, ref, self.ss.at[slot], self.rs.at[slot], target)
        copy.start()
        self.sent.append(copy)

    def own(self):
        p, me = self.p, self.p.t
        for s, d in DIRS:
            self.send(SLOT["zA" + s], me, None, "A", p.at(0, d))
        self.send(SLOT["xB"], me, None, "B", p.at(1, 0))
        self.send(2 * N_ICI, me, None, None, p.at(0, 0, True))
        for s, d in DIRS:
            self.send(SLOT["zB" + s], me, None, "B", p.at(0, d))
        self.send(SLOT["xA0"], me, None, "A", p.at(1, 0))

    def take(self, *names):
        for name in names:
            self.take_one(name)

    def take_one(self, name):
        p = self.p
        dx, dz, half, part = ARRIVE[name]
        member = p.member(dx, dz)
        ref = self.ref(member, half, part)
        remote(ref, ref, self.ss.at[SLOT[name]], self.rs.at[SLOT[name]], p.at(1, 0)).wait_recv()
        kind, s = name[:2], name[2:]
        if name == "xB":
            for s2, d in DIRS:
                self.send(SLOT["zX" + s2], member, None, "B", p.at(0, d))
        if kind[0] == "z":
            d = 1 if s == "+" else -1
            if kind == "zA":
                self.send(SLOT["xA" + s], member, None, "A", p.at(1, 0))
            self.send(SLOT["h" + kind[1] + s], member, 0 if d > 0 else 1, part, p.at(0, d))
        if kind == "hA":
            self.send(SLOT["xh" + s], member, half, "A", p.at(1, 0))
        self.send(N_ICI + SLOT[name], member, half, part, p.at(0, 0, True))

    def twin(self, *names):
        for name in names:
            if name == "own":
                slot, ref = 2 * N_ICI, self.ref(self.p.member(0, 0, True), None, None)
            else:
                dx, dz, half, part = ARRIVE[name]
                slot, ref = N_ICI + SLOT[name], self.ref(self.p.member(dx, dz, True), half, part)
            remote(ref, ref, self.ss.at[slot], self.rs.at[slot], self.p.at(0, 0, True)).wait_recv()

    def finish(self):
        for copy in self.sent:
            copy.wait_send()


NEAR = ("own", "xB", "xA0", "zA+", "zA-", "zB+", "zB-")
MID = ("zX+", "zX-", "xA+", "xA-")
FAR = ("hA+", "hA-", "hB+", "hB-", "hX+", "hX-", "xh+", "xh-")


def positions(ids, slots, counts):
    own = jnp.zeros(ids.shape, jnp.int32)
    experts = counts.shape[1]
    for e in range(experts):
        own = own + jnp.where(ids == e, counts[0, e], 0)
    live = (ids < experts) & (slots < own)
    return jnp.where(live, ids * CAP + slots, -1)


def silu_parts(gate):
    sigma = jax.nn.sigmoid(gate)
    return gate * sigma, sigma * (1.0 + gate * (1.0 - sigma))


def forward_kernel(
    tok, grd, ids, slots, counts, score, gpre, upre, wds, wg, wu, wd,
    dgu, wpart, bk, ggate, gup, gdown,
    G, T, R, SB, RV, gp_v, up_v, wds_v, wg_v, wu_v, wd_v, dguT, hidT, acc_gu, acc_d,
    rgu, rguT, rhT, BP, BR, CS, MS, ggo, gdo,
    lsem, gss, grs, tss, trs, rss, rrs, ass, ars, bss, brs, dss, drs,
):
    p = Place()
    g, t, c = p.g, p.t, p.c
    peers = [((g + k) % 8, t) for k in range(1, 8)]
    loads = [
        pltpu.make_async_copy(grd, G.at[t], lsem.at[0]),
        pltpu.make_async_copy(tok, T.at[t], lsem.at[1]),
        pltpu.make_async_copy(wds, wds_v, lsem.at[2]),
        pltpu.make_async_copy(gpre, gp_v, lsem.at[3]),
        pltpu.make_async_copy(upre, up_v, lsem.at[4]),
        pltpu.make_async_copy(wg.at[0], wg_v, lsem.at[5]),
        pltpu.make_async_copy(wu.at[0], wu_v, lsem.at[6]),
        pltpu.make_async_copy(wd.at[0], wd_v, lsem.at[7]),
    ]
    for copy in loads:
        copy.start()
    greet([p.at(0, 1), p.at(0, -1), p.at(1, 0), p.at(0, 0, True)] + peers)
    gg = Gather(p, G, CUT, gss, grs)
    tg = Gather(p, T, CUT, tss, trs)
    rg = Gather(p, R, CUT, rss, rrs)
    loads[0].wait()
    gg.own()
    loads[1].wait()

    pos = positions(ids[...], slots[...], counts)
    n = SB.shape[0] * 16
    row = lax.broadcasted_iota(jnp.int32, (n, 128), 0)
    want = (row // 16) * CAP + row % CAP
    pick = pos == want
    scale = jnp.sum(jnp.where(pick, score[...], 0.0), axis=1, keepdims=True)
    pick = pick.astype(F32).astype(BF)
    wide = T.shape[2] // 2
    low = lax.broadcasted_iota(jnp.int32, (n, wide), 0) % 16 < 8
    grad = lax.broadcasted_iota(jnp.int32, (n, wide), 0) % 8 >= CAP
    vals_t = jnp.where(low, dot_nn(pick, T[t, :, 0:wide]), dot_nn(pick, T[t, :, wide:])) * scale
    vals_g = jnp.where(low, dot_nn(pick, G[t, :, 0:wide]), dot_nn(pick, G[t, :, wide:]))
    SB[...] = jnp.where(grad, vals_g, vals_t).astype(BF).reshape(SB.shape)
    sends = []
    for k in range(1, 8):
        e = (g + k) % 8
        copy = remote(SB.at[e], RV.at[g], ass.at[k], ars.at[k], (e, t))
        copy.start()
        sends.append(copy)
    RV[pl.ds(g, 1)] = SB[pl.ds(g, 1)]
    acc_d[...] = jnp.zeros_like(acc_d)
    acc_gu[...] = jnp.zeros_like(acc_gu)

    gg.take("xB", "zA+", "zA-")
    for k in range(1, 8):
        src = (g + 8 - k) % 8
        remote(SB.at[src], RV.at[src], ass.at[k], ars.at[k], (src, t)).wait_recv()
    rows = lax.broadcasted_iota(jnp.int32, (R.shape[1], n), 0)
    cols = lax.broadcasted_iota(jnp.int32, (R.shape[1], n), 1)
    base = ((rows % 32) // CAP) * 16 + (rows // 32) * CAP + rows % CAP
    got = RV[...].reshape(n, wide)
    R[t, :, 0:wide] = dot_nn((cols == base).astype(F32).astype(BF), got).astype(BF)
    R[t, :, wide:] = dot_nn((cols == base + 8).astype(F32).astype(BF), got).astype(BF)
    rg.own()
    gg.take("zB+", "zB-", "xA0", "zX+", "zX-")
    rg.take("xB", "zA+", "zA-")
    gg.take("hA+", "hA-", "xA+", "xA-")
    tg.own()
    rg.take("zB+", "zB-", "xA0", "zX+", "zX-")
    gg.take("hB+", "hB-", "hX+", "hX-", "xh+", "xh-")
    rg.take("hA+", "hA-", "xA+", "xA-")
    tg.take("xB")
    gg.twin(*NEAR, *MID, *FAR)
    for copy in loads[2:5]:
        copy.wait()

    def g_unit(j, carry):
        two = pl.ds(2 * j, 2)
        toks = pl.ds(pl.multiple_of(j * 256, 256), 256)
        h = dot_nt(G[two].reshape(256, G.shape[2]), wds_v[...])
        gate, up = gp_v[toks].astype(F32), up_v[toks].astype(F32)
        silu, slope = silu_parts(gate)
        dg, du = h * up * slope, h * silu
        dgu[two, :, 0:256] = dg.astype(BF).reshape(2, 128, 256)
        dgu[two, :, 256:512] = du.astype(BF).reshape(2, 128, 256)
        dguT[j, 0:256] = dg.T.astype(BF)
        dguT[j, 256:512] = du.T.astype(BF)
        hidT[...] = (silu * up).T.astype(BF)

        def part(i, carry):
            cs = pl.ds(pl.multiple_of(i * 512, 512), 512)
            acc_d[:, cs] += dot_nn(hidT[...], G[two, :, cs].reshape(256, 512))
            return carry

        return lax.fori_loop(0, G.shape[2] // 512, part, carry)

    def t_unit(j):
        two = pl.ds(2 * j, 2)

        def part(i, carry):
            cs = pl.ds(pl.multiple_of(i * 512, 512), 512)
            acc_gu[:, cs] += dot_nn(dguT[j], T[two, :, cs].reshape(256, 512))
            return carry

        lax.fori_loop(0, T.shape[2] // 512, part, 0)

    lax.fori_loop(0, 3, g_unit, 0)
    rg.take("hB+", "hB-", "hX+", "hX-", "xh+", "xh-")
    tg.take("zA+", "zA-")
    lax.fori_loop(3, 8, g_unit, 0)
    rg.twin(*NEAR, *MID, *FAR)
    tg.take("zB+", "zB-")
    for copy in loads[5:8]:
        copy.wait()

    def r_unit(m, carry):
        mem = pl.ds(8 * m, 8)
        rin = R[mem, 0:32].reshape(256, R.shape[2])
        rgr = R[mem, 32:64].reshape(256, R.shape[2])
        gate, up = dot_nn(rin, wg_v[...]), dot_nn(rin, wu_v[...])
        h = dot_nt(rgr, wd_v[...])
        silu, slope = silu_parts(gate)
        dg, du = h * up * slope, h * silu
        dgb, dub = dg.astype(BF), du.astype(BF)
        at = pl.ds(pl.multiple_of(m * 256, 256), 256)
        rgu[at, 0:256] = dgb
        rgu[at, 256:512] = dub
        rguT[0:256, at] = dg.T.astype(BF)
        rguT[256:512, at] = du.T.astype(BF)
        rhT[:, at] = (silu * up).T.astype(BF)
        q = jnp.sum(dgb.astype(F32) * gate + dub.astype(F32) * up, axis=1, keepdims=True)
        hi = q.astype(BF).astype(F32)
        lane = lax.broadcasted_iota(jnp.int32, (256, 128), 1)
        tail = jnp.where(lane == 0, hi, jnp.where(lane == 1, q - hi, 0.0)).astype(BF)
        BP[pl.ds(4 * m, 4), :, :, R.shape[2] :] = tail.reshape(4, 2, 32, 128)
        return carry

    lax.fori_loop(0, 2, r_unit, 0)

    def b_unit(i, carry):
        cs = pl.ds(pl.multiple_of(i * 512, 512), 512)
        out = dot_nt(rgu[:, 0:256], wg_v[cs]) + dot_nt(rgu[:, 256:512], wu_v[cs])
        BP[:, :, :, cs] = out.astype(BF).reshape(8, 2, 32, 512)
        return carry

    lax.fori_loop(0, R.shape[2] // 512, b_unit, 0)
    across = remote(BP.at[:, 1 - c], BR, dss.at[0], drs.at[0], p.at(0, 0, True))
    across.start()
    tg.take("xA0", "zX+", "zX-")

    def w_unit(i, carry):
        cs = pl.ds(pl.multiple_of(i * 256, 256), 256)
        rin = R[:, 0:32, cs].reshape(512, 256)
        rgr = R[:, 32:64, cs].reshape(512, 256)
        gu = dot_nn(rguT[...], rin)
        ggo[0, cs] = gu[0:256].T.astype(BF)
        ggo[1, cs] = gu[256:512].T.astype(BF)
        gdo[:, cs] = dot_nn(rhT[...], rgr).astype(BF)
        return carry

    remote(BP.at[:, c], BR, dss.at[0], drs.at[0], p.at(0, 0, True)).wait_recv()

    def s_unit(i, carry):
        CS[pl.ds(i, 1)] = (BP[pl.ds(i, 1), c].astype(F32) + BR[pl.ds(i, 1)].astype(F32)).astype(BF)
        return carry

    lax.fori_loop(0, 8, s_unit, 0)
    r0 = lax.broadcasted_iota(jnp.int32, (256, 256), 0)
    r1 = lax.broadcasted_iota(jnp.int32, (256, 256), 1)
    turn = (r1 == ((r0 // CAP) % 8) * 32 + (r0 // 32) * CAP + r0 % CAP).astype(F32).astype(BF)
    MS[...] = dot_nn(turn, CS[...].reshape(256, CS.shape[2])).astype(BF).reshape(MS.shape)
    for k in range(1, 8):
        e = (g + k) % 8
        copy = remote(MS.at[e], bk.at[g], bss.at[k], brs.at[k], (e, t))
        copy.start()
        sends.append(copy)
    keep = pltpu.make_async_copy(MS.at[g], bk.at[g], lsem.at[8])
    keep.start()
    tg.take("hA+", "hA-", "xA+", "xA-")
    lax.fori_loop(0, R.shape[2] // 256, w_unit, 0)
    outs = [
        pltpu.make_async_copy(ggo.at[0], ggate.at[0], lsem.at[9]),
        pltpu.make_async_copy(ggo.at[1], gup.at[0], lsem.at[10]),
        pltpu.make_async_copy(gdo, gdown.at[0], lsem.at[11]),
    ]
    for copy in outs:
        copy.start()
    tg.twin(*NEAR)
    t_unit(p.chip(0, 0))
    t_unit(p.chip(1, 0))
    t_unit(p.chip(0, 1))
    t_unit(p.chip(0, -1))
    tg.take("hB+", "hB-", "hX+", "hX-", "xh+", "xh-")
    tg.twin(*MID)
    t_unit(p.chip(1, 1))
    t_unit(p.chip(1, -1))
    tg.twin(*FAR)
    t_unit(p.chip(0, 2))
    t_unit(p.chip(1, 2))

    def turn_unit(i, carry):
        cs = pl.ds(pl.multiple_of(i * 256, 256), 256)
        wpart[0, cs] = acc_gu[0:256, cs].T.astype(BF)
        wpart[1, cs] = acc_gu[256:512, cs].T.astype(BF)
        wpart[2, cs] = acc_d[:, cs].T.astype(BF)
        return carry

    lax.fori_loop(0, T.shape[2] // 256, turn_unit, 0)
    keep.wait()
    for copy in outs:
        copy.wait()
    for k in range(1, 8):
        src = (g + 8 - k) % 8
        remote(MS.at[src], bk.at[src], bss.at[k], brs.at[k], (src, t)).wait_recv()
    across.wait_send()
    for copy in sends:
        copy.wait_send()
    gg.finish()
    tg.finish()
    rg.finish()


CUT = 1152
RCUT = 768


def reduce_kernel(
    dgu, wgs, wus, bk, wpart, ids, slots, counts, score,
    gtok, gscore, gw,
    S, DS, DR, XA, ZH, ZF, XB, W, WH, WF, WX, info, mine, QS, QR,
    lsem, dss, drs, xss, xrs, zss, zrs, wss, wrs, iss, irs, qss, qrs,
):
    p = Place()
    c = p.c
    width = gtok.shape[1]
    load = pltpu.make_async_copy(wpart, W, lsem.at[0])
    load.start()
    chips = [(dx, dz) for dx in range(2) for dz in range(4) if (dx, dz) != (0, 0)]
    greet(
        [p.at(dx, dz) for dx, dz in chips]
        + [p.at(0, 0, True), p.over(0, 1), p.over(0, -1), p.over(1, 0)]
    )
    sends = []

    def ship(src, dst, ss, rs, target):
        copy = remote(src, dst, ss, rs, target)
        copy.start()
        sends.append(copy)

    def land(ref, ss, rs):
        remote(ref, ref, ss, rs, p.at(0, 0, True)).wait_recv()

    pos = positions(ids[...], slots[...], counts)
    which = lax.broadcasted_iota(jnp.int32, (8, 128), 0)
    mine[...] = jnp.where(which == 0, pos.astype(F32), score[...])
    for i, (dx, dz) in enumerate(chips):
        ship(mine, info.at[dx, (4 - dz) % 4], iss.at[i], irs.at[i], p.at(dx, dz))
    info[0, 0] = mine[...]

    load.wait()
    half = (pl.ds(0, 160), pl.ds(160, 160))
    for dh in range(2):
        for i, (s, d) in enumerate(DIRS):
            ship(W.at[:, p.group(dh, 2), half[i]], WH.at[dh, i], wss.at[dh, i], wrs.at[dh, i], p.over(0, d))

    def weights_second():
        for dh in (1, 0):
            for i, (s, d) in enumerate(DIRS):
                land(WH.at[dh, i], wss.at[dh, i], wrs.at[dh, i])
                at = p.group(dh, d)
                for a in range(3):
                    W[a, at, half[i]] = (W[a, at, half[i]].astype(F32) + WH[dh, i, a].astype(F32)).astype(BF)
                ship(W.at[:, at], WF.at[dh, i], wss.at[dh, 2 + i], wrs.at[dh, 2 + i], p.over(0, d))

    def weights_third():
        for i in range(2):
            land(WF.at[1, i], wss.at[1, 2 + i], wrs.at[1, 2 + i])
        at = p.group(1, 0)
        for a in range(3):
            total = W[a, at].astype(F32) + WF[1, 0, a].astype(F32) + WF[1, 1, a].astype(F32)
            W[a, at] = total.astype(BF)
        ship(W.at[:, at], WX, wss.at[0, 4], wrs.at[0, 4], p.over(1, 0))

    def weights_last():
        for i in range(2):
            land(WF.at[0, i], wss.at[0, 2 + i], wrs.at[0, 2 + i])
        land(WX, wss.at[0, 4], wrs.at[0, 4])
        at = p.group(0, 0)
        for a in range(3):
            total = W[a, at].astype(F32) + WF[0, 0, a].astype(F32) + WF[0, 1, a].astype(F32) + WX[a].astype(F32)
            gw[a] = total.astype(BF)

    def make(dx, dz):
        j = p.chip(dx, dz)
        slot = dx * 4 + dz

        def part(i, carry):
            cs = pl.ds(pl.multiple_of(i * 512, 512), 512)
            two = dgu[pl.ds(2 * j, 2)].reshape(256, 512)
            out = dot_nt(two[:, 0:256], wgs[cs]) + dot_nt(two[:, 256:512], wus[cs])
            DS[slot, :, :, cs] = out.astype(BF).reshape(2, 128, 512)
            return carry

        lax.fori_loop(0, width // 512, part, 0)
        ship(DS.at[slot, 1 - c], DR.at[slot], dss.at[slot], drs.at[slot], p.at(0, 0, True))

    row = lax.broadcasted_iota(jnp.int32, (256, 128), 0)
    want = ((row // 32) * CAP + row % CAP).astype(F32)

    def join(dx, dz, first):
        j = p.chip(dx, dz)
        slot = dx * 4 + dz
        if (dx, dz) != (0, 0):
            i = chips.index((dx, (4 - dz) % 4))
            land(info.at[dx, dz], iss.at[i], irs.at[i])
        pick = (want == info[dx, dz, 0:1]) & ((row // CAP) % 8 == j)
        scale = jnp.sum(jnp.where(pick, info[dx, dz, 1:2], 0.0), axis=1, keepdims=True)
        pickT = pick.astype(F32).T.astype(BF)
        pick = pick.astype(F32).astype(BF)
        q = dot_tn(bk[:, :, width:].reshape(256, 128), pick)
        QS[dx, dz] = jnp.broadcast_to(q[0:1] + q[1:2], (8, 128))
        land(DR.at[slot], dss.at[slot], drs.at[slot])

        def part(i, carry):
            cs = pl.ds(pl.multiple_of(i * 512, 512), 512)
            rows = (bk[:, :, cs].reshape(256, 512).astype(F32) * scale).astype(BF)
            total = dot_nn(pickT, rows) + DS[slot, c, :, cs].astype(F32) + DR[slot, :, cs].astype(F32)
            S[slot, :, cs] = total.astype(BF)
            return carry

        lax.fori_loop(0, width // 512, part, 0)
        if (dx, dz) != (0, 0):
            i = chips.index((dx, dz))
            ship(QS.at[dx, dz], QR.at[i], qss.at[i], qrs.at[i], p.at(dx, dz))

    colA, colB = pl.ds(0, RCUT), pl.ds(RCUT, width - RCUT)
    rowh = (pl.ds(0, 64), pl.ds(64, 64))

    def cols_of(lane):
        return colA if lane == 2 else colB

    def box(ref, lane, *idx):
        return ref.at[(lane,) + idx + (pl.ds(0, RCUT if lane == 2 else width - RCUT),)]

    def z_first(lane):
        slot = (lane % 2) * 4 + 2
        for i, (s, d) in enumerate(DIRS):
            ship(S.at[slot, rowh[i], cols_of(lane)], box(ZH, lane, i, pl.ds(0, 64)), zss.at[lane, i], zrs.at[lane, i], p.at(0, d))

    def z_second(lane):
        for i, (s, d) in enumerate(DIRS):
            slot = (lane % 2) * 4 + d % 4
            ref = box(ZH, lane, i, pl.ds(0, 64))
            land(ref, zss.at[lane, i], zrs.at[lane, i])
            S[slot, rowh[i], cols_of(lane)] = (
                S[slot, rowh[i], cols_of(lane)].astype(F32) + ref[...].astype(F32)
            ).astype(BF)
            ship(S.at[slot, :, cols_of(lane)], box(ZF, lane, i, pl.ds(0, 128)), zss.at[lane, 2 + i], zrs.at[lane, 2 + i], p.at(0, d))

    def z_third(lane):
        for i in range(2):
            land(box(ZF, lane, i, pl.ds(0, 128)), zss.at[lane, 2 + i], zrs.at[lane, 2 + i])
        slot = (lane % 2) * 4
        return (
            S[slot, :, cols_of(lane)].astype(F32)
            + box(ZF, lane, 0, pl.ds(0, 128))[...].astype(F32)
            + box(ZF, lane, 1, pl.ds(0, 128))[...].astype(F32)
        )

    def x_send(dz):
        ship(S.at[4 + dz, :, colA], XA.at[dz], xss.at[dz], xrs.at[dz], p.at(1, 0))

    def x_add(dz):
        land(XA.at[dz], xss.at[dz], xrs.at[dz])
        S[dz, :, colA] = (S[dz, :, colA].astype(F32) + XA[dz].astype(F32)).astype(BF)

    make(1, 2)
    make(0, 2)
    join(1, 2, True)
    x_send(2)
    z_first(1)
    make(1, 1)
    join(0, 2, True)
    z_first(0)
    make(1, 3)
    join(1, 1, True)
    x_send(1)
    make(0, 1)
    join(1, 3, True)
    x_send(3)
    x_add(2)
    z_first(2)
    make(0, 3)
    z_second(1)
    join(0, 1, True)
    make(1, 0)
    join(0, 3, True)
    z_second(0)
    weights_second()
    join(1, 0, True)
    x_send(0)
    make(0, 0)
    x_add(1)
    x_add(3)
    z_second(2)
    join(0, 0, True)
    S[4, :, colB] = z_third(1).astype(BF)
    ship(S.at[4, :, colB], XB, xss.at[4], xrs.at[4], p.at(1, 0))
    weights_third()
    partB = z_third(0)
    land(XB, xss.at[4], xrs.at[4])
    gtok[:, colB] = (partB + XB[...].astype(F32)).astype(BF)
    x_add_last = XA.at[0]
    land(x_add_last, xss.at[0], xrs.at[0])
    gtok[:, colA] = (z_third(2) + XA[0].astype(F32)).astype(BF)
    total = QS[0, 0]
    for i, (dx, dz) in enumerate(chips):
        land(QR.at[i], qss.at[i], qrs.at[i])
        total = total + QR[i]
    gscore[...] = total / score[...]
    weights_last()
    for copy in sends:
        copy.wait_send()


def shards(
    tokens, grad_out, route_score, expert_ids, slots, counts, shared_gate_pre, shared_up_pre,
    shared_w_gate, shared_w_up, shared_w_down, w_gate, w_up, w_down,
):
    tok_dev, width = tokens.shape
    ff = w_gate.shape[2]
    ids, slt, score = (a.reshape(1, tok_dev) for a in (expert_ids, slots, route_score))
    dma = pltpu.SemaphoreType.DMA
    wide = width + 128
    dgu, wpart, bk, ggate, gup, gdown = pl.pallas_call(
        forward_kernel,
        out_shape=(
            jax.ShapeDtypeStruct((16, tok_dev, 2 * ff), BF),
            jax.ShapeDtypeStruct((3, width, ff), BF),
            jax.ShapeDtypeStruct((8, 32, wide), BF),
            jax.ShapeDtypeStruct((1, width, ff), BF),
            jax.ShapeDtypeStruct((1, width, ff), BF),
            jax.ShapeDtypeStruct((1, ff, width), BF),
        ),
        in_specs=[ANY, ANY, VM, VM, SM, VM, ANY, ANY, ANY, ANY, ANY, ANY],
        out_specs=(VM, VM, ANY, ANY, ANY, ANY),
        scratch_shapes=[
            pltpu.VMEM((16, tok_dev, width), BF),
            pltpu.VMEM((16, tok_dev, width), BF),
            pltpu.VMEM((16, 64, width), BF),
            pltpu.VMEM((8, 16, width // 2), BF),
            pltpu.VMEM((8, 16, width // 2), BF),
            pltpu.VMEM((16 * tok_dev, ff), BF),
            pltpu.VMEM((16 * tok_dev, ff), BF),
            pltpu.VMEM((ff, width), BF),
            pltpu.VMEM((width, ff), BF),
            pltpu.VMEM((width, ff), BF),
            pltpu.VMEM((ff, width), BF),
            pltpu.VMEM((8, 2 * ff, 256), BF),
            pltpu.VMEM((ff, 256), BF),
            pltpu.VMEM((2 * ff, width), F32),
            pltpu.VMEM((ff, width), F32),
            pltpu.VMEM((512, 2 * ff), BF),
            pltpu.VMEM((2 * ff, 512), BF),
            pltpu.VMEM((ff, 512), BF),
            pltpu.VMEM((8, 2, 32, wide), BF),
            pltpu.VMEM((8, 32, wide), BF),
            pltpu.VMEM((8, 32, wide), BF),
            pltpu.VMEM((8, 32, wide), BF),
            pltpu.VMEM((2, width, ff), BF),
            pltpu.VMEM((ff, width), BF),
            dma((12,)),
            dma((N_SLOT,)), dma((N_SLOT,)),
            dma((N_SLOT,)), dma((N_SLOT,)),
            dma((N_SLOT,)), dma((N_SLOT,)),
            dma((8,)), dma((8,)),
            dma((8,)), dma((8,)),
            dma((1,)), dma((1,)),
        ],
        compiler_params=pltpu.CompilerParams(
            collective_id=0, has_side_effects=True, vmem_limit_bytes=63 << 20
        ),
    )(
        tokens, grad_out, ids, slt, counts, score, shared_gate_pre, shared_up_pre,
        shared_w_down, w_gate, w_up, w_down,
    )
    gtok, gscore, gw = pl.pallas_call(
        reduce_kernel,
        out_shape=(
            jax.ShapeDtypeStruct((tok_dev, width), BF),
            jax.ShapeDtypeStruct((8, tok_dev), F32),
            jax.ShapeDtypeStruct((3, width // 8, ff), BF),
        ),
        in_specs=[VM, VM, VM, VM, ANY, VM, VM, SM, VM],
        out_specs=(VM, VM, VM),
        scratch_shapes=[
            pltpu.VMEM((8, tok_dev, width), BF),
            pltpu.VMEM((8, 2, tok_dev, width), BF),
            pltpu.VMEM((8, tok_dev, width), BF),
            pltpu.VMEM((4, tok_dev, RCUT), BF),
            pltpu.VMEM((3, 2, 64, width - RCUT), BF),
            pltpu.VMEM((3, 2, tok_dev, width - RCUT), BF),
            pltpu.VMEM((tok_dev, width - RCUT), BF),
            pltpu.VMEM((3, 8, width // 8, ff), BF),
            pltpu.VMEM((2, 2, 3, width // 16, ff), BF),
            pltpu.VMEM((2, 2, 3, width // 8, ff), BF),
            pltpu.VMEM((3, width // 8, ff), BF),
            pltpu.VMEM((2, 4, 8, 128), F32),
            pltpu.VMEM((8, 128), F32),
            pltpu.VMEM((2, 4, 8, 128), F32),
            pltpu.VMEM((7, 8, 128), F32),
            dma((1,)),
            dma((8,)), dma((8,)),
            dma((5,)), dma((5,)),
            dma((3, 4)), dma((3, 4)),
            dma((2, 5)), dma((2, 5)),
            dma((7,)), dma((7,)),
            dma((7,)), dma((7,)),
        ],
        compiler_params=pltpu.CompilerParams(
            collective_id=1, has_side_effects=True, vmem_limit_bytes=63 << 20
        ),
    )(
        dgu, shared_w_gate, shared_w_up, bk, wpart.reshape(3, 8, width // 8, ff), ids, slt, counts, score,
    )
    return (gtok, gscore[0], gw[0], gw[1], gw[2].T, ggate, gup, gdown)


def solution(mesh):
    placed = (
        P(("grp", "tp"), None),
        P(("grp", "tp"), None),
        P(("grp", "tp")),
        P(("grp", "tp")),
        P(("grp", "tp")),
        P(("grp", "tp"), None),
        P("grp", "tp"),
        P("grp", "tp"),
        P(None, "tp"),
        P(None, "tp"),
        P("tp", None),
        P("grp", None, "tp"),
        P("grp", None, "tp"),
        P("grp", "tp", None),
    )
    return jax.shard_map(
        shards,
        mesh=mesh,
        in_specs=placed,
        out_specs=(
            P(("grp", "tp"), None),
            P(("grp", "tp")),
            P("grp", "tp"),
            P("grp", "tp"),
            P("tp", "grp"),
            P("grp", None, "tp"),
            P("grp", None, "tp"),
            P("grp", "tp", None),
        ),
        check_vma=False,
    )
```

time: 538 us -> 202 us (0.38)
  waiting for transfers between devices: 384 us -> 0 us
  Pallas kernels: 0 us -> 191 us
  matrix products: 81.1 us -> 0 us
  starting transfers between devices: 24.3 us -> 0 us
  local copies, waits for them, and re-layouts: 28.9 us -> 9.74 us
  between operations: 14.4 us -> 0.67 us
    pallas_call x0 -> x2, Pallas kernels: none -> 191 us  [the longest x1 126 us: shards(): pl.pallas_call(forward_kernel, out_shape=(jax.ShapeDtypeStruct((16, tok_d...]
    unnamed x8 -> x0, waiting for transfers between devices: 154 us -> none
    all_to_all x3 -> x0, waiting for transfers between devices: 98.5 us -> none  [the longest x1 43.7 us: shards(): lax.all_to_all(wide_grad, ('grp', 'tp'), split_axis=0, concat_axis=0, til...]
    dot_general x17 -> x0, matrix products: 81.1 us -> none  [the longest x6 37 us: contract_cols(): lax.dot_general(left, right, (((1,), (1,)), ((), ())), preferred_element_...]
    reduce_scatter x2 -> x0, waiting for transfers between devices: 66.2 us -> none  [the longest x1 66.2 us: shards(): lax.psum_scatter(part_down.astype(jnp.bfloat16), 'grp', scatter_dimension...]
    all_gather x2 -> x0, waiting for transfers between devices: 65.3 us -> none  [the longest x1 65.3 us: shards(): lax.all_gather(grad_out, 'tp', axis=0, tiled=True)]
    all_to_all x3 -> x0, starting transfers between devices: 23.7 us -> none  [the longest x1 9.63 us: shards(): lax.all_to_all(wide_grad, ('grp', 'tp'), split_axis=0, concat_axis=0, til...]
    reshape x3 -> x0, local copies, waits for them, and re-layouts: 16.3 us -> none  [the longest x1 5.6 us: shards(): partial_value.astype(jnp.bfloat16).reshape(sources, CAP, width)]
  transfers between devices with their start and end apart: 9 -> 0, of which waited for: 7 -> 0; matrix products, arithmetic and copies ran while one was open for 21% -> 0% of each run, Pallas kernels for 0% -> 0%
where the time goes in v1:
time: 202 us; the launch traced here: 201 us
  Pallas kernels  191 us (95%)
  local copies, waits for them, and re-layouts  9.74 us (5%)
    pallas_call x1, Pallas kernels, shards(): pl.pallas_call(forward_kernel, out_shape=(jax.ShapeDtypeStruct((16, tok_d...  126 us
    pallas_call x1, Pallas kernels, shards(): pl.pallas_call(reduce_kernel, out_shape=(jax.ShapeDtypeStruct((tok_dev, w...  64.8 us
    unnamed x10, local copies, waits for them, and re-layouts  6.6 us

profile of v1, /device:TPU:6, one launch (start us, length us, event | category | flops | bytes accessed | tf_op | source)
XLA Modules:
  0.0 201.4 jit_solution(4765387618242291641)
XLA Ops:
  0.6 126.2 %shard_map.197 = (bf16[16,128,512]{2,1,0:T(8,128)(2,1)}, bf16[3,2560,256]{2,1,0:T(8,128)(2,1)}, bf16[8,32,2688]{2,1,0:T(8,128)(2,1)}, bf16[1,2560,256]{2,1,0:T(8...) custom-call(bf16[128,2560]{1,0:T(8,128)(2,1)} %tok.1, bf16[128,2560]{1,0:T(8,128)(2,1)} %grd.1, ...), custom_call_target="tpu_custom_call" | custom-call | tf_op jit(solution)/shard_map/pallas_call | solution.py:605
  126.8 64.8 %shard_map.198 = (bf16[128,2560]{1,0:T(8,128)(2,1)}, f32[8,128]{1,0:T(8,128)}, bf16[3,320,256]{2,1,0:T(8,128)(2,1)}) custom-call(bf16[16,128,512]{2,1,0:T(8,128)(2,1)} %get-tuple-element.17.dgu, bf16[2560,256]{1,0:T(8,128)(2,1)} %wgs.1, bf16[2560,256]{1,0:T(8,128)(2,1)} %wus.1, bf16[8,32,2688]{2,1,0:T(8,128)(2,1)} %get-tuple-element.18.bk, ...), custom_call_target="tpu_custom_call" | custom-call | tf_op jit(solution)/shard_map/pallas_call | solution.py:657
  191.6 0.0 copy-start.2
  191.6 1.3 slice_bitcast_fusion.3
  192.9 1.9 slice_bitcast_fusion
  194.8 2.0 copy.26
  196.7 0.0 copy-done.2
  196.7 0.0 copy-start.1
  196.7 1.1 copy.27
  197.8 0.7 copy-done.1
  198.5 0.0 copy-start
  198.5 1.1 copy.28
  199.6 0.7 copy-done
  200.3 1.1 copy.29
Async XLA Ops:
  191.6 5.1 %copy-start.2 = (bf16[1,2560,256]{2,1,0:T(8,128)(2,1)S(1)}, bf16[1,2560,256]{2,1,0:T(8,128)(2,1)}, u32[]{:S(2)}) copy-start(bf16[1,2560,256]{2,1,0:T(8,128)(2,1)} %get-tuple-element.42) | copy-start | bytes 3932164
  196.7 1.8 copy-start.1
  198.5 1.8 copy-start

commit v2 on v0

v2 whole, which is shorter than its diff:
```python
import functools

import jax
import jax.numpy as jnp
from jax import lax
from jax.experimental import pallas as pl
from jax.experimental.pallas import tpu as pltpu
from jax.sharding import PartitionSpec as P

CAP = 4
MESH = pl.DeviceIdType.MESH
BF, F32 = jnp.bfloat16, jnp.float32
ANY = pl.BlockSpec(memory_space=pl.ANY)
VM = pl.BlockSpec(memory_space=pltpu.VMEM)
SM = pl.BlockSpec(memory_space=pltpu.SMEM)
DIRS = (("+", 1), ("-", -1))


def dot_nn(a, b):
    return lax.dot_general(a, b, (((1,), (0,)), ((), ())), preferred_element_type=F32)


def dot_nt(a, b):
    return lax.dot_general(a, b, (((1,), (1,)), ((), ())), preferred_element_type=F32)


def dot_tn(a, b):
    return lax.dot_general(a, b, (((0,), (0,)), ((), ())), preferred_element_type=F32)


class Place:
    def __init__(self):
        self.g = lax.axis_index("grp")
        self.t = lax.axis_index("tp")
        self.xh, self.y = self.g // 4, self.g % 4
        self.xl, self.z, self.c = self.t // 8, (self.t // 2) % 4, self.t % 2

    def chip(self, dx, dz):
        return ((self.xl + dx) % 2) * 4 + (self.z + dz + 4) % 4

    def member(self, dx, dz, other=False):
        core = 1 - self.c if other else self.c
        return self.chip(dx, dz) * 2 + core

    def at(self, dx, dz, other=False):
        return (self.g, self.member(dx, dz, other))

    def group(self, dh, dy):
        return ((self.xh + dh) % 2) * 4 + (self.y + dy + 4) % 4

    def over(self, dh, dy):
        return (self.group(dh, dy), self.t)

    def peer(self, dh, dy):
        return (self.group(dh, dy), (self.t + 8 * dh) % 16)


def greet(targets):
    barrier = pltpu.get_barrier_semaphore()
    for target in targets:
        pl.semaphore_signal(barrier, inc=1, device_id=target, device_id_type=MESH)
    pl.semaphore_wait(barrier, len(targets))


def remote(src, dst, ss, rs, target):
    return pltpu.make_async_remote_copy(
        src_ref=src, dst_ref=dst, send_sem=ss, recv_sem=rs, device_id=target, device_id_type=MESH
    )


ARRIVE = {"xB": (1, 0, None, "B"), "xA0": (1, 0, None, "A")}
for _s, _d in DIRS:
    _h = 0 if _d > 0 else 1
    ARRIVE["zA" + _s] = (0, -_d, None, "A")
    ARRIVE["zB" + _s] = (0, -_d, None, "B")
    ARRIVE["zX" + _s] = (1, -_d, None, "B")
    ARRIVE["hA" + _s] = (0, 2, _h, "A")
    ARRIVE["hB" + _s] = (0, 2, _h, "B")
    ARRIVE["hX" + _s] = (1, 2, _h, "B")
    ARRIVE["xA" + _s] = (1, -_d, None, "A")
    ARRIVE["xh" + _s] = (1, 2, _h, "A")
SLOT = {name: i for i, name in enumerate(ARRIVE)}
N_ICI = len(SLOT)
N_SLOT = 2 * N_ICI + 1


class Gather:
    def __init__(self, place, buf, cut, ss, rs):
        self.p, self.buf, self.cut, self.ss, self.rs = place, buf, cut, ss, rs
        self.rows, self.width = buf.shape[1], buf.shape[2]
        self.sent = {}

    def ref(self, member, half, part):
        rows = pl.ds(0, self.rows) if half is None else pl.ds(half * (self.rows // 2), self.rows // 2)
        cols = {
            None: pl.ds(0, self.width),
            "A": pl.ds(0, self.cut),
            "B": pl.ds(self.cut, self.width - self.cut),
        }[part]
        return self.buf.at[member, rows, cols]

    def send(self, slot, chip, half, part, target):
        ref = self.ref(self.p.member(*chip), half, part)
        copy = remote(ref, ref, self.ss.at[slot], self.rs.at[slot], target)
        copy.start()
        self.sent.setdefault((chip[0], chip[1] % 4), []).append(copy)

    def own(self):
        p, me = self.p, (0, 0)
        for s, d in DIRS:
            self.send(SLOT["zA" + s], me, None, "A", p.at(0, d))
        self.send(SLOT["xB"], me, None, "B", p.at(1, 0))
        self.send(2 * N_ICI, me, None, None, p.at(0, 0, True))

    def own_rest(self):
        p, me = self.p, (0, 0)
        for s, d in DIRS:
            self.send(SLOT["zB" + s], me, None, "B", p.at(0, d))
        self.send(SLOT["xA0"], me, None, "A", p.at(1, 0))

    def take(self, *names):
        for name in names:
            self.take_one(name)

    def take_one(self, name):
        p = self.p
        dx, dz, half, part = ARRIVE[name]
        member = (dx, dz)
        ref = self.ref(p.member(dx, dz), half, part)
        remote(ref, ref, self.ss.at[SLOT[name]], self.rs.at[SLOT[name]], p.at(1, 0)).wait_recv()
        kind, s = name[:2], name[2:]
        if name == "xB":
            for s2, d in DIRS:
                self.send(SLOT["zX" + s2], member, None, "B", p.at(0, d))
        if kind[0] == "z":
            d = 1 if s == "+" else -1
            if kind == "zA":
                self.send(SLOT["xA" + s], member, None, "A", p.at(1, 0))
            self.send(SLOT["h" + kind[1] + s], member, 0 if d > 0 else 1, part, p.at(0, d))
        if kind == "hA":
            self.send(SLOT["xh" + s], member, half, "A", p.at(1, 0))
        self.send(N_ICI + SLOT[name], member, half, part, p.at(0, 0, True))

    def twin(self, *names):
        for name in names:
            if name == "own":
                slot, ref = 2 * N_ICI, self.ref(self.p.member(0, 0, True), None, None)
            else:
                dx, dz, half, part = ARRIVE[name]
                slot, ref = N_ICI + SLOT[name], self.ref(self.p.member(dx, dz, True), half, part)
            remote(ref, ref, self.ss.at[slot], self.rs.at[slot], self.p.at(0, 0, True)).wait_recv()

    def finish(self, chip=None):
        for key in list(self.sent) if chip is None else [(chip[0], chip[1] % 4)]:
            for copy in self.sent.pop(key, []):
                copy.wait_send()


CHIP = ((0, 0), (1, 0), (0, -1), (0, 1), (1, -1), (1, 1), (0, 2), (1, 2))
NEED = (
    ("own",),
    ("xB", "xA0"),
    ("zA+", "zB+"),
    ("zA-", "zB-"),
    ("zX+", "xA+"),
    ("zX-", "xA-"),
    ("hA+", "hA-", "hB+", "hB-"),
    ("hX+", "hX-", "xh+", "xh-"),
)
PEERS = [(dh, dy) for dh in range(2) for dy in range(4) if (dh, dy) != (0, 0)]
MATES = [(dx, dz) for dx in range(2) for dz in range(4) if (dx, dz) != (0, 0)]
CUT = 1152
RCUT = 1024
ORDER = (
    "G0", "g2", "Rown", "r2", "rzA+", "rzA-", "rxB", "M00", "rzB-", "rzB+", "rhA+", "rhA-", "rxA0",
    "rzX+", "rzX-", "rhB+", "rhB-", "rxA+", "rxA-", "rxh+", "gzA+", "gzA-", "gxB", "gzB+", "gzB-",
    "gxA0", "rxh-", "rhX+", "rhX-", "R0", "Town", "R1", "Rb", "L0", "G1", "ghA+", "ghA-", "t2", "G2",
    "T0", "ghB+", "Rs", "ghB-", "G3", "Rw0", "gxA+", "gxA-", "G6", "Rw1", "Rf", "M01", "gzX+", "gzX-",
    "tzA+", "tzA-", "M03", "gxh+", "gxh-", "N01", "N03", "N00", "M02", "N02", "G4", "tzB+", "tzB-",
    "G5", "M10", "N10", "J01", "J03", "thA+", "txB", "thA-", "ghX+", "ghX-", "J02", "J00", "txA0",
    "J10", "L2", "thB+", "L3", "M11", "thB-", "N11", "G7", "T2", "T3", "J11", "Z10", "S1", "S0", "L1",
    "tzX+", "L6", "tzX-", "D0", "M12", "N12", "M13", "N13", "T1", "txh+", "txA+", "T6", "txA-", "txh-",
    "J12", "Z11", "S2", "J13", "S3", "L4", "D1", "thX+", "thX-", "Z20", "L5", "T4", "L7", "T5", "Z21",
    "T7", "W0", "D2", "X1", "W0b", "W11", "W10", "X2", "Z12", "X3", "D3", "Z31", "Z22", "W2", "F0",
    "F2", "W3",
)


def positions(ids, slots, counts):
    own = jnp.zeros(ids.shape, jnp.int32)
    experts = counts.shape[1]
    for e in range(experts):
        own = own + jnp.where(ids == e, counts[0, e], 0)
    live = (ids < experts) & (slots < own)
    return jnp.where(live, ids * CAP + slots, -1)


def silu_parts(gate):
    sigma = jax.nn.sigmoid(gate)
    return gate * sigma, sigma * (1.0 + gate * (1.0 - sigma))


def kernel(
    tok, grd, ids, slots, counts, score, gpre, upre, wds, wgs, wus, wg, wu, wd,
    gtok, gscore, gsg, gsd, ggate, gup, gdown, TH,
    G, R, TV, SB, RV, dg_v, du_v, wds_v, wgs_v, wus_v, wg_v, wu_v, wd_v, dguT, hidT, acc_gu, acc_d,
    rgu, rguT, rhT, BP, BR, MS, BK, WS, W, WH, WF, WX, WD, DH, DF, DX,
    XA, ZH, ZF, XB, info, mine, QS, QR,
    lsem, tsem, wsem, gss, grs, tss, trs, rss, rrs, ass, ars, bss, brs, dss, drs, css, crs,
    xss, xrs, zss, zrs, wss, wrs, hss, hrs, iss, irs, qss, qrs, credit,
):
    p = Place()
    g, t, c = p.g, p.t, p.c
    width = gtok.shape[1]
    pieces = ((grd, G.at[t]), (tok, TV.at[0, 0]), (TV.at[0, 0], TH.at[t]), (wds, wds_v), (gpre, dg_v), (upre, du_v),
              (wg.at[0], wg_v), (wu.at[0], wu_v), (wd.at[0], wd_v), (wgs, wgs_v), (wus, wus_v))
    loads = [pltpu.make_async_copy(a, b, lsem.at[i]) for i, (a, b) in enumerate(pieces)]
    for i, copy in enumerate(loads):
        if i != 2:
            copy.start()
    greet(
        [p.at(dx, dz) for dx, dz in MATES]
        + [p.at(0, 0, True)]
        + [p.peer(dh, dy) for dh, dy in PEERS]
        + [p.over(1, 0)]
    )
    gg = Gather(p, G, CUT, gss, grs)
    tg = Gather(p, TH, CUT, tss, trs)
    rg = Gather(p, R, CUT, rss, rrs)
    gathers = {"g": gg, "t": tg, "r": rg}
    sends = []

    def ship(src, dst, ss, rs, target):
        copy = remote(src, dst, ss, rs, target)
        copy.start()
        sends.append(copy)

    def land(ref, ss, rs):
        remote(ref, ref, ss, rs, p.at(0, 0, True)).wait_recv()

    loads[0].wait()
    gg.own()
    loads[1].wait()
    loads[2].start()

    pos = positions(ids[...], slots[...], counts)
    n = SB.shape[0] * 16
    row = lax.broadcasted_iota(jnp.int32, (n, 128), 0)
    pick = pos == (row // 16) * CAP + row % CAP
    scale = jnp.sum(jnp.where(pick, score[...], 0.0), axis=1, keepdims=True)
    pick = pick.astype(F32).astype(BF)
    wide = width // 2
    low = lax.broadcasted_iota(jnp.int32, (n, wide), 0) % 16 < 8
    grad = lax.broadcasted_iota(jnp.int32, (n, wide), 0) % 8 >= CAP
    vals_t = jnp.where(low, dot_nn(pick, TV[0, 0, :, 0:wide]), dot_nn(pick, TV[0, 0, :, wide:])) * scale
    vals_g = jnp.where(low, dot_nn(pick, G[t, :, 0:wide]), dot_nn(pick, G[t, :, wide:]))
    SB[...] = jnp.where(grad, vals_g, vals_t).astype(BF).reshape(SB.shape)
    for i, (dh, dy) in enumerate(PEERS):
        ship(SB.at[p.group(dh, dy)], RV.at[g], ass.at[i], ars.at[i], p.peer(dh, dy))
    RV[pl.ds(g, 1)] = SB[pl.ds(g, 1)]
    which = lax.broadcasted_iota(jnp.int32, (8, 128), 0)
    mine[...] = jnp.where(which == 0, pos.astype(F32), score[...])
    for i, (dx, dz) in enumerate(MATES):
        ship(mine, info.at[dx, (4 - dz) % 4], iss.at[i], irs.at[i], p.at(dx, dz))
    info[0, 0] = mine[...]
    acc_d[...] = jnp.zeros_like(acc_d)
    acc_gu[...] = jnp.zeros_like(acc_gu)

    def cols(i, size):
        return pl.ds(pl.multiple_of(i * size, size), size)

    def rows_own():
        for i, (dh, dy) in enumerate(PEERS):
            land(RV.at[p.group(dh, -dy)], ass.at[i], ars.at[i])
        rows = lax.broadcasted_iota(jnp.int32, (R.shape[1], n), 0)
        at = lax.broadcasted_iota(jnp.int32, (R.shape[1], n), 1)
        base = ((rows % 32) // CAP) * 16 + (rows // 32) * CAP + rows % CAP
        got = RV[...].reshape(n, wide)
        R[t, :, 0:wide] = dot_nn((at == base).astype(F32).astype(BF), got).astype(BF)
        R[t, :, wide:] = dot_nn((at == base + 8).astype(F32).astype(BF), got).astype(BF)
        rg.own()

    def shared_unit(i):
        gg.twin(*NEED[i])
        for k in (3, 4, 5):
            if loads[k] is not None:
                loads[k].wait()
                loads[k] = None
        j = p.chip(*CHIP[i])
        two = pl.ds(2 * j, 2)
        toks = pl.ds(pl.multiple_of(j * 256, 256), 256)
        h = dot_nt(G[two].reshape(256, width), wds_v[...])
        gate, up = dg_v[toks].astype(F32), du_v[toks].astype(F32)
        silu, slope = silu_parts(gate)
        dg, du = h * up * slope, h * silu
        dg_v[toks] = dg.astype(BF)
        du_v[toks] = du.astype(BF)
        dguT[j, 0:256] = dg.T.astype(BF)
        dguT[j, 256:512] = du.T.astype(BF)
        hidT[...] = (silu * up).T.astype(BF)

        def part(k, carry):
            cs = cols(k, 512)
            acc_d[:, cs] += dot_nn(hidT[...], G[two, :, cs].reshape(256, 512))
            return carry

        lax.fori_loop(0, width // 512, part, 0)

    slot_of, free = {}, [0, 1]

    def token_load(i):
        slot_of[i] = free.pop(0)
        tg.twin(*NEED[i])
        token_copy(i).start()

    def token_copy(i):
        j = p.chip(*CHIP[i])
        return pltpu.make_async_copy(TH.at[pl.ds(2 * j, 2)], TV.at[slot_of[i]], tsem.at[slot_of[i]])

    def token_unit(i):
        token_copy(i).wait()
        j, slot = p.chip(*CHIP[i]), slot_of[i]

        def part(k, carry):
            cs = cols(k, 512)
            acc_gu[:, cs] += dot_nn(dguT[j], TV[slot, :, :, cs].reshape(256, 512))
            return carry

        lax.fori_loop(0, width // 512, part, 0)
        free.append(slot)

    def r_unit(m):
        if m == 0:
            for i in range(8):
                rg.twin(*NEED[i])
            for k in (6, 7, 8):
                loads[k].wait()
        rin = R[8 * m : 8 * m + 8, 0:32].reshape(256, width)
        rgr = R[8 * m : 8 * m + 8, 32:64].reshape(256, width)
        gate, up = dot_nn(rin, wg_v[...]), dot_nn(rin, wu_v[...])
        h = dot_nt(rgr, wd_v[...])
        silu, slope = silu_parts(gate)
        dg, du = h * up * slope, h * silu
        dgb, dub = dg.astype(BF), du.astype(BF)
        at = pl.ds(m * 256, 256)
        rgu[at, 0:256] = dgb
        rgu[at, 256:512] = dub
        rguT[0:256, at] = dg.T.astype(BF)
        rguT[256:512, at] = du.T.astype(BF)
        rhT[:, at] = (silu * up).T.astype(BF)
        q = jnp.sum(dgb.astype(F32) * gate + dub.astype(F32) * up, axis=1, keepdims=True)
        hi = q.astype(BF).astype(F32)
        lane = lax.broadcasted_iota(jnp.int32, (256, 128), 1)
        tail = jnp.where(lane == 0, hi, jnp.where(lane == 1, q - hi, 0.0)).astype(BF)
        BP[4 * m : 4 * m + 4, :, :, width:] = tail.reshape(4, 2, 32, 128)

    def r_back():
        def part(k, carry):
            cs = cols(k, 512)
            out = dot_nt(rgu[:, 0:256], wg_v[cs]) + dot_nt(rgu[:, 256:512], wu_v[cs])
            BP[:, :, :, cs] = out.astype(BF).reshape(8, 2, 32, 512)
            return carry

        lax.fori_loop(0, width // 512, part, 0)
        ship(BP.at[:, 1 - c], BR, dss.at[0], drs.at[0], p.at(0, 0, True))

    keep = pltpu.make_async_copy(MS.at[g], BK.at[g], lsem.at[11])

    def r_send():
        land(BR, dss.at[0], drs.at[0])

        def part(k, carry):
            one = pl.ds(k, 1)
            BP[one, c] = (BP[one, c].astype(F32) + BR[one].astype(F32)).astype(BF)
            return carry

        lax.fori_loop(0, 8, part, 0)
        r0 = lax.broadcasted_iota(jnp.int32, (256, 256), 0)
        r1 = lax.broadcasted_iota(jnp.int32, (256, 256), 1)
        home, group = (r0 // CAP) % 8, r0 // 32
        held = jnp.where(group // 4 == p.xh, home, (home + 4) % 8)
        turn = (r1 == held * 32 + group * CAP + r0 % CAP).astype(F32).astype(BF)
        MS[...] = dot_nn(turn, BP[:, c].reshape(256, BP.shape[3])).astype(BF).reshape(MS.shape)
        for i, (dh, dy) in enumerate(PEERS):
            ship(MS.at[p.group(dh, dy)], BK.at[g], bss.at[i], brs.at[i], p.peer(dh, dy))
        keep.start()

    def w_copies(k, slot):
        return (
            pltpu.make_async_copy(WS.at[slot, 0], ggate.at[0, cols(k, 256)], wsem.at[slot, 0]),
            pltpu.make_async_copy(WS.at[slot, 1], gup.at[0, cols(k, 256)], wsem.at[slot, 1]),
            pltpu.make_async_copy(WS.at[slot, 2], gdown.at[0, :, cols(k, 256)], wsem.at[slot, 2]),
        )

    def w_unit(k, carry):
        slot = k % 2

        @pl.when(k >= 2)
        def _():
            for copy in w_copies(k - 2, slot):
                copy.wait()

        cs = cols(k, 256)
        gu = dot_nn(rguT[...], R[:, 0:32, cs].reshape(512, 256))
        WS[slot, 0] = gu[0:256].T.astype(BF)
        WS[slot, 1] = gu[256:512].T.astype(BF)
        WS[slot, 2] = dot_nn(rhT[...], R[:, 32:64, cs].reshape(512, 256)).astype(BF)
        for copy in w_copies(k, slot):
            copy.start()
        return carry

    def r_free():
        rg.finish()
        pl.semaphore_signal(credit, inc=1, device_id=p.at(0, 0, True), device_id_type=MESH)

    half = (pl.ds(0, 160), pl.ds(160, 160))

    def sum_first(V, VH, ss, rs, *dhs):
        for dh in dhs:
            for i, (s, d) in enumerate(DIRS):
                ship(V.at[:, p.group(dh, 2), half[i]], VH.at[dh, i], ss.at[dh, i], rs.at[dh, i], p.over(0, d))

    def sum_second(V, VH, VF, ss, rs, dh):
        for i, (s, d) in enumerate(DIRS):
            land(VH.at[dh, i], ss.at[dh, i], rs.at[dh, i])
            at = p.group(dh, d)
            for a in range(V.shape[0]):
                V[a, at, half[i]] = (V[a, at, half[i]].astype(F32) + VH[dh, i, a].astype(F32)).astype(BF)
            ship(V.at[:, at], VF.at[dh, i], ss.at[dh, 2 + i], rs.at[dh, 2 + i], p.over(0, d))

    def sum_total(V, VF, ss, rs, dh, a):
        return V[a, p.group(dh, 0)].astype(F32) + VF[dh, 0, a].astype(F32) + VF[dh, 1, a].astype(F32)

    def sum_third(V, VF, VX, ss, rs):
        for i in range(2):
            land(VF.at[1, i], ss.at[1, 2 + i], rs.at[1, 2 + i])
        at = p.group(1, 0)
        for a in range(V.shape[0]):
            V[a, at] = sum_total(V, VF, ss, rs, 1, a).astype(BF)
        ship(V.at[:, at], VX, ss.at[0, 4], rs.at[0, 4], p.over(1, 0))

    def sum_last(V, VF, VX, ss, rs):
        for i in range(2):
            land(VF.at[0, i], ss.at[0, 2 + i], rs.at[0, 2 + i])
        land(VX, ss.at[0, 4], rs.at[0, 4])
        return [sum_total(V, VF, ss, rs, 0, a) + VX[a].astype(F32) for a in range(V.shape[0])]

    def turn(acc, V):
        def part(k, carry):
            for a in range(V.shape[0]):
                block = acc[256 * a : 256 * a + 256, cols(k, 640)].T.astype(BF)
                V[a, 2 * k] = block[0:320]
                V[a, 2 * k + 1] = block[320:640]
            return carry

        lax.fori_loop(0, width // 640, part, 0)

    def down_last():
        total = sum_last(WD, DF, DX, hss, hrs)[0]
        gsd[...] = total.astype(BF)

    def weights_last():
        for a, total in enumerate(sum_last(W, WF, WX, wss, wrs)):
            gsg[a] = total.astype(BF)

    seen = set()

    def share(dx, dz):
        if "load" not in seen:
            seen.add("load")
            loads[9].wait()
            loads[10].wait()
        gg.finish((dx, dz))
        j = p.chip(dx, dz)
        toks = pl.ds(pl.multiple_of(j * 256, 256), 256)

        def part(k, carry):
            cs = cols(k, 512)
            out = dot_nt(dg_v[toks], wgs_v[cs]) + dot_nt(du_v[toks], wus_v[cs])
            G[pl.ds(2 * j, 2), :, cs] = out.astype(BF).reshape(2, 128, 512)
            return carry

        lax.fori_loop(0, width // 512, part, 0)

    def swap(dx, dz):
        if "credit" not in seen:
            seen.add("credit")
            pl.semaphore_wait(credit, 1)
        for h in range(2):
            at = 2 * (dx * 4 + dz) + h
            ship(G.at[p.member(dx, dz, True), pl.ds(64 * h, 64)], R.at[at], css.at[at], crs.at[at], p.at(0, 0, True))

    def picked(dx, dz):
        row = lax.broadcasted_iota(jnp.int32, (256, 128), 0)
        want = ((row // 32) * CAP + row % CAP).astype(F32)
        return (want == info[dx, dz, 0:1]) & ((row // CAP) % 8 == p.chip(dx, dz))

    def join(dx, dz):
        if "back" not in seen:
            seen.add("back")
            for i, (dh, dy) in enumerate(PEERS):
                land(BK.at[p.group(dh, -dy)], bss.at[i], brs.at[i])
            keep.wait()
            for i, (ax, az) in enumerate(MATES):
                land(info.at[ax, (4 - az) % 4], iss.at[i], irs.at[i])
            scale = jnp.zeros((256, 1), F32)
            for ax in range(2):
                for az in range(4):
                    scale += jnp.sum(jnp.where(picked(ax, az), info[ax, az, 1:2], 0.0), axis=1, keepdims=True)

            def weigh(k, carry):
                cs = cols(k, 512)
                BK[:, :, cs] = (BK[:, :, cs].reshape(256, 512).astype(F32) * scale).astype(BF).reshape(8, 32, 512)
                return carry

            lax.fori_loop(0, width // 512, weigh, 0)
        slot, me = dx * 4 + dz, p.member(dx, dz)
        pick = picked(dx, dz).astype(F32)
        pickT, pick = pick.T.astype(BF), pick.astype(BF)
        q = dot_tn(BK[:, :, width:].reshape(256, 128), pick)
        QS[dx, dz] = jnp.broadcast_to(q[0:1] + q[1:2], (8, 128))
        if (dx, dz) != (0, 0):
            i = MATES.index((dx, dz))
            ship(QS.at[dx, dz], QR.at[i], qss.at[i], qrs.at[i], p.at(dx, dz))
        for h in range(2):
            land(R.at[2 * slot + h], css.at[2 * slot + h], crs.at[2 * slot + h])

        def part(k, carry):
            cs = cols(k, 512)
            other = R[2 * slot : 2 * slot + 2, :, cs].reshape(128, 512)
            total = dot_nn(pickT, BK[:, :, cs].reshape(256, 512)) + G[me, :, cs].astype(F32) + other.astype(F32)
            G[me, :, cs] = total.astype(BF)
            return carry

        lax.fori_loop(0, width // 512, part, 0)

    colA, colB = pl.ds(0, RCUT), pl.ds(RCUT, width - RCUT)
    rowh = (pl.ds(0, 64), pl.ds(64, 64))

    def cols_of(lane):
        return colA if lane == 2 else colB

    def box(ref, lane, i, rows):
        return ref.at[lane, i, pl.ds(0, rows), pl.ds(0, RCUT if lane == 2 else width - RCUT)]

    def z_first(lane):
        me = p.member(lane % 2, 2)
        for i, (s, d) in enumerate(DIRS):
            ship(G.at[me, rowh[i], cols_of(lane)], box(ZH, lane, i, 64), zss.at[lane, i], zrs.at[lane, i], p.at(0, d))

    def z_second(lane):
        for i, (s, d) in enumerate(DIRS):
            me = p.member(lane % 2, d)
            ref = box(ZH, lane, i, 64)
            land(ref, zss.at[lane, i], zrs.at[lane, i])
            G[me, rowh[i], cols_of(lane)] = (
                G[me, rowh[i], cols_of(lane)].astype(F32) + ref[...].astype(F32)
            ).astype(BF)
            ship(G.at[me, :, cols_of(lane)], box(ZF, lane, i, 128), zss.at[lane, 2 + i], zrs.at[lane, 2 + i], p.at(0, d))

    def z_third(lane):
        for i in range(2):
            land(box(ZF, lane, i, 128), zss.at[lane, 2 + i], zrs.at[lane, 2 + i])
        return (
            G[p.member(lane % 2, 0), :, cols_of(lane)].astype(F32)
            + box(ZF, lane, 0, 128)[...].astype(F32)
            + box(ZF, lane, 1, 128)[...].astype(F32)
        )

    def x_send(dz):
        ship(G.at[p.member(1, dz), :, colA], XA.at[dz], xss.at[dz], xrs.at[dz], p.at(1, 0))

    def x_add(dz):
        land(XA.at[dz], xss.at[dz], xrs.at[dz])
        me = p.member(0, dz)
        G[me, :, colA] = (G[me, :, colA].astype(F32) + XA[dz].astype(F32)).astype(BF)

    def z_cross():
        me = p.member(1, 0)
        G[me, :, colB] = z_third(1).astype(BF)
        ship(G.at[me, :, colB], XB, xss.at[4], xrs.at[4], p.at(1, 0))

    def out_b():
        total = z_third(0)
        land(XB, xss.at[4], xrs.at[4])
        gtok[:, colB] = (total + XB[...].astype(F32)).astype(BF)

    def out_a():
        land(XA.at[0], xss.at[0], xrs.at[0])
        gtok[:, colA] = (z_third(2) + XA[0].astype(F32)).astype(BF)

    def tokens_own():
        loads[2].wait()
        tg.own()

    fixed = {
        "Rown": rows_own, "Town": tokens_own, "g2": gg.own_rest, "t2": tg.own_rest, "r2": rg.own_rest, "Rb": r_back, "Rs": r_send, "Rf": r_free,
        "Rw0": lambda: lax.fori_loop(0, 5, w_unit, 0), "Rw1": lambda: lax.fori_loop(5, 10, w_unit, 0),
        "D0": lambda: (turn(acc_d, WD), sum_first(WD, DH, hss, hrs, 1, 0)),
        "D1": lambda: (sum_second(WD, DH, DF, hss, hrs, 1), sum_second(WD, DH, DF, hss, hrs, 0)),
        "D2": lambda: sum_third(WD, DF, DX, hss, hrs), "D3": down_last,
        "W0": lambda: (turn(acc_gu, W), sum_first(W, WH, wss, wrs, 1)),
        "W0b": lambda: sum_first(W, WH, wss, wrs, 0),
        "W11": lambda: sum_second(W, WH, WF, wss, wrs, 1), "W10": lambda: sum_second(W, WH, WF, wss, wrs, 0),
        "W2": lambda: sum_third(W, WF, WX, wss, wrs), "W3": weights_last,
        "Z31": z_cross, "F0": out_b, "F2": out_a,
    }
    for step in ORDER:
        if step in fixed:
            fixed[step]()
        elif step[0] in gathers:
            gathers[step[0]].take(step[1:])
        elif step[:2] in ("Z1", "Z2"):
            (z_first if step[1] == "1" else z_second)(int(step[2]))
        else:
            unit = {"G": shared_unit, "L": token_load, "T": token_unit, "R": r_unit, "S": x_send, "X": x_add, "M": share, "N": swap, "J": join}
            unit[step[0]](*(int(k) for k in step[1:]))
    total = QS[0, 0]
    for i in range(len(MATES)):
        land(QR.at[i], qss.at[i], qrs.at[i])
        total = total + QR[i]
    gscore[...] = total[0:1] / score[...]
    for k in (8, 9):
        for copy in w_copies(k, k % 2):
            copy.wait()
    for copy in sends:
        copy.wait_send()
    gg.finish()
    tg.finish()


def store_kernel(gtok, gscore, gsg, gsd, ggate, gup, gdown, *rest):
    parts = (ggate, gup, gdown, gtok, gsg.at[0], gsg.at[1], gsd, gscore)
    outs, held, (first, second) = rest[:8], rest[8:16], rest[16:]
    loads = [pltpu.make_async_copy(a, b, first.at[i]) for i, (a, b) in enumerate(zip(parts, held))]
    stores = [pltpu.make_async_copy(a, b, second.at[i]) for i, (a, b) in enumerate(zip(held, outs))]
    for copy in loads:
        copy.start()
    for load, store in zip(loads, stores):
        load.wait()
        store.start()
    for copy in stores:
        copy.wait()


def shards(
    tokens, grad_out, route_score, expert_ids, slots, counts, shared_gate_pre, shared_up_pre,
    shared_w_gate, shared_w_up, shared_w_down, w_gate, w_up, w_down,
):
    tok_dev, width = tokens.shape
    ff = w_gate.shape[2]
    ids, slt, score = (a.reshape(1, tok_dev) for a in (expert_ids, slots, route_score))
    dma = pltpu.SemaphoreType.DMA
    wide, rows = width + 128, width // 8
    most = max(RCUT, width - RCUT)

    def vm(*shape, dtype=BF):
        return pltpu.VMEM(shape, dtype)

    def out(*shape, dtype=BF):
        return jax.ShapeDtypeStruct(shape, dtype)

    gtok, gscore, gsg, gsd, ggate, gup, gdown, _ = pl.pallas_call(
        kernel,
        out_shape=(
            out(tok_dev, width), out(1, tok_dev, dtype=F32), out(2, rows, ff), out(rows, ff),
            out(1, width, ff), out(1, width, ff), out(1, ff, width), out(16, tok_dev, width),
        ),
        in_specs=[ANY, ANY, VM, VM, SM, VM] + [ANY] * 8,
        out_specs=(VM, VM, VM, VM, ANY, ANY, ANY, ANY),
        scratch_shapes=[
            vm(16, tok_dev, width), vm(16, 64, width), vm(2, 2, tok_dev, width),
            vm(8, 16, width // 2), vm(8, 16, width // 2),
            vm(16 * tok_dev, ff), vm(16 * tok_dev, ff),
            vm(ff, width), vm(width, ff), vm(width, ff), vm(width, ff), vm(width, ff), vm(ff, width),
            vm(8, 2 * ff, 256), vm(ff, 256), vm(2 * ff, width, dtype=F32), vm(ff, width, dtype=F32),
            vm(512, 2 * ff), vm(2 * ff, 512), vm(ff, 512),
            vm(8, 2, 32, wide), vm(8, 32, wide), vm(8, 32, wide), vm(8, 32, wide),
            vm(2, 3, 256, 256),
            vm(2, 8, rows, ff), vm(2, 2, 2, rows // 2, ff), vm(2, 2, 2, rows, ff), vm(2, rows, ff),
            vm(1, 8, rows, ff), vm(2, 2, 1, rows // 2, ff), vm(2, 2, 1, rows, ff), vm(1, rows, ff),
            vm(4, tok_dev, RCUT), vm(3, 2, tok_dev // 2, most), vm(3, 2, tok_dev, most), vm(tok_dev, width - RCUT),
            vm(2, 4, 8, 128, dtype=F32), vm(8, 128, dtype=F32), vm(2, 4, 8, 128, dtype=F32), vm(7, 8, 128, dtype=F32),
            dma((12,)), dma((2,)), dma((2, 3)),
            dma((N_SLOT,)), dma((N_SLOT,)), dma((N_SLOT,)), dma((N_SLOT,)), dma((N_SLOT,)), dma((N_SLOT,)),
            dma((7,)), dma((7,)), dma((7,)), dma((7,)), dma((1,)), dma((1,)), dma((16,)), dma((16,)),
            dma((5,)), dma((5,)), dma((3, 4)), dma((3, 4)), dma((2, 5)), dma((2, 5)), dma((2, 5)), dma((2, 5)),
            dma((7,)), dma((7,)), dma((7,)), dma((7,)), pltpu.SemaphoreType.REGULAR,
        ],
        compiler_params=pltpu.CompilerParams(
            collective_id=0, has_side_effects=True, vmem_limit_bytes=63 << 20
        ),
    )(
        tokens, grad_out, ids, slt, counts, score, shared_gate_pre, shared_up_pre,
        shared_w_down, shared_w_gate, shared_w_up, w_gate, w_up, w_down,
    )
    shapes = (
        ((1, width, ff), BF), ((1, width, ff), BF), ((1, ff, width), BF), ((tok_dev, width), BF),
        ((rows, ff), BF), ((rows, ff), BF), ((rows, ff), BF), ((1, tok_dev), F32),
    )
    ggate, gup, gdown, gtok, gsg, gsu, gsd, gscore = pl.pallas_call(
        store_kernel,
        out_shape=tuple(out(*shape, dtype=dtype) for shape, dtype in shapes),
        in_specs=[ANY] * 7,
        out_specs=(ANY,) * 8,
        scratch_shapes=[vm(*shape, dtype=dtype) for shape, dtype in shapes] + [dma((8,)), dma((8,))],
        compiler_params=pltpu.CompilerParams(vmem_limit_bytes=63 << 20),
    )(gtok, gscore, gsg, gsd, ggate, gup, gdown)
    return (gtok, gscore.reshape(tok_dev), gsg, gsu, gsd.T, ggate, gup, gdown)


def solution(mesh):
    placed = (
        P(("grp", "tp"), None),
        P(("grp", "tp"), None),
        P(("grp", "tp")),
        P(("grp", "tp")),
        P(("grp", "tp")),
        P(("grp", "tp"), None),
        P("grp", "tp"),
        P("grp", "tp"),
        P(None, "tp"),
        P(None, "tp"),
        P("tp", None),
        P("grp", None, "tp"),
        P("grp", None, "tp"),
        P("grp", "tp", None),
    )
    return jax.shard_map(
        shards,
        mesh=mesh,
        in_specs=placed,
        out_specs=(
            P(("grp", "tp"), None),
            P(("grp", "tp")),
            P("grp", "tp"),
            P("grp", "tp"),
            P("tp", "grp"),
            P("grp", None, "tp"),
            P("grp", None, "tp"),
            P("grp", "tp", None),
        ),
        check_vma=False,
    )
```

time: 538 us -> 150 us (0.28)
  waiting for transfers between devices: 384 us -> 0 us
  Pallas kernels: 0 us -> 149 us
  matrix products: 81.1 us -> 0 us
  local copies, waits for them, and re-layouts: 28.9 us -> 0 us
  starting transfers between devices: 24.3 us -> 0 us
  between operations: 14.4 us -> 0.81 us
    unnamed x8 -> x0, waiting for transfers between devices: 154 us -> none
    pallas_call x0 -> x2, Pallas kernels: none -> 149 us  [the longest x1 146 us: shards(): pl.pallas_call(kernel, out_shape=(out(tok_dev, width), out(1, tok_dev, dt...]
    all_to_all x3 -> x0, waiting for transfers between devices: 98.5 us -> none  [the longest x1 43.7 us: shards(): lax.all_to_all(wide_grad, ('grp', 'tp'), split_axis=0, concat_axis=0, til...]
    dot_general x17 -> x0, matrix products: 81.1 us -> none  [the longest x6 37 us: contract_cols(): lax.dot_general(left, right, (((1,), (1,)), ((), ())), preferred_element_...]
    reduce_scatter x2 -> x0, waiting for transfers between devices: 66.2 us -> none  [the longest x1 66.2 us: shards(): lax.psum_scatter(part_down.astype(jnp.bfloat16), 'grp', scatter_dimension...]
    all_gather x2 -> x0, waiting for transfers between devices: 65.3 us -> none  [the longest x1 65.3 us: shards(): lax.all_gather(grad_out, 'tp', axis=0, tiled=True)]
    all_to_all x3 -> x0, starting transfers between devices: 23.7 us -> none  [the longest x1 9.63 us: shards(): lax.all_to_all(wide_grad, ('grp', 'tp'), split_axis=0, concat_axis=0, til...]
    reshape x3 -> x0, local copies, waits for them, and re-layouts: 16.3 us -> none  [the longest x1 5.6 us: shards(): partial_value.astype(jnp.bfloat16).reshape(sources, CAP, width)]
  transfers between devices with their start and end apart: 9 -> 0, of which waited for: 7 -> 0; matrix products, arithmetic and copies ran while one was open for 21% -> 0% of each run, Pallas kernels for 0% -> 0%
where the time goes in v2:
time: 150 us
  Pallas kernels  149 us (99%)
    pallas_call x1, Pallas kernels, shards(): pl.pallas_call(kernel, out_shape=(out(tok_dev, width), out(1, tok_dev, dt...  146 us
    pallas_call x1, Pallas kernels, shards(): pl.pallas_call(store_kernel, out_shape=tuple((out(*shape, dtype=dtype) fo...  3.74 us

profile of v2, /device:TPU:6, one launch (start us, length us, event | category | flops | bytes accessed | tf_op | source)
XLA Modules:
  0.0 150.2 jit_solution(14721130226449346000)
XLA Ops:
  0.6 145.7 %shard_map.197 = (bf16[128,2560]{1,0:T(8,128)(2,1)}, f32[1,128]{1,0:T(1,128)}, bf16[2,320,256]{2,1,0:T(8,128)(2,1)}, bf16[320,256]{1,0:T(8,128)(2,1)}, bf16[1,25...) custom-call(bf16[128,2560]{1,0:T(8,128)(2,1)} %tok.1, ...), custom_call_target="tpu_custom_call" | custom-call | tf_op jit(solution)/shard_map/pallas_call | solution.py:663
  146.3 3.7 %shard_map.198 = (bf16[1,2560,256]{2,1,0:T(8,128)(2,1)}, bf16[1,2560,256]{2,1,0:T(8,128)(2,1)}, bf16[1,256,2560]{2,1,0:T(8,128)(2,1)}, bf16[128,2560]{1,0:T(8,12...) custom-call(bf16[128,2560]{1,0:T(8,128)(2,1)} %get-tuple-element.23., ...), custom_call_target="tpu_custom_call" | custom-call | tf_op jit(solution)/shard_map/pallas_call | solution.py:701

commit v3 on v2

--- a/solution.py
+++ b/solution.py
@@ -172,17 +172,16 @@
 CUT = 1152
 RCUT = 1024
 ORDER = (
-    "G0", "g2", "Rown", "r2", "rzA+", "rzA-", "rxB", "M00", "rzB-", "rzB+", "rhA+", "rhA-", "rxA0",
-    "rzX+", "rzX-", "rhB+", "rhB-", "rxA+", "rxA-", "rxh+", "gzA+", "gzA-", "gxB", "gzB+", "gzB-",
-    "gxA0", "rxh-", "rhX+", "rhX-", "R0", "Town", "R1", "Rb", "L0", "G1", "ghA+", "ghA-", "t2", "G2",
-    "T0", "ghB+", "Rs", "ghB-", "G3", "Rw0", "gxA+", "gxA-", "G6", "Rw1", "Rf", "M01", "gzX+", "gzX-",
-    "tzA+", "tzA-", "M03", "gxh+", "gxh-", "N01", "N03", "N00", "M02", "N02", "G4", "tzB+", "tzB-",
-    "G5", "M10", "N10", "J01", "J03", "thA+", "txB", "thA-", "ghX+", "ghX-", "J02", "J00", "txA0",
-    "J10", "L2", "thB+", "L3", "M11", "thB-", "N11", "G7", "T2", "T3", "J11", "Z10", "S1", "S0", "L1",
-    "tzX+", "L6", "tzX-", "D0", "M12", "N12", "M13", "N13", "T1", "txh+", "txA+", "T6", "txA-", "txh-",
-    "J12", "Z11", "S2", "J13", "S3", "L4", "D1", "thX+", "thX-", "Z20", "L5", "T4", "L7", "T5", "Z21",
-    "T7", "W0", "D2", "X1", "W0b", "W11", "W10", "X2", "Z12", "X3", "D3", "Z31", "Z22", "W2", "F0",
-    "F2", "W3",
+    "G0", "g2", "Rown", "r2", "rzA+", "rzA-", "rxB", "M00", "gzA+", "gzB-", "gzA-", "gzB+", "rhA-",
+    "rzB-", "rzB+", "gxA0", "rxA-", "gxB", "rzX-", "rzX+", "rhA+", "G1", "G2", "rxA+", "rxA0", "ghA-",
+    "Town", "t2", "rhB-", "G3", "ghA+", "ghB+", "rhX+", "rxh+", "ghB-", "rxh-", "rhB+", "rhX-", "R0",
+    "R1", "Rb", "Rh", "M03", "G6", "gzX+", "gxA+", "gzX-", "gxA-", "Rs", "tzA-", "tzA+", "gxh-", "Rf",
+    "M02", "M10", "N10", "M01", "tzB+", "N01", "tzB-", "gxh+", "G4", "N00", "ghX+", "N02", "G5", "txB",
+    "N03", "L1", "M11", "ghX-", "txA0", "thA+", "N11", "M13", "N13", "thB-", "T1", "J02", "L0", "thA-",
+    "Z10", "G7", "D0", "M12", "N12", "J11", "S1", "tzX+", "txA+", "tzX-", "J13", "txA-", "T0", "thB+",
+    "J12", "Z11", "S2", "D1", "txh+", "L2", "J00", "txh-", "thX-", "thX+", "S3", "T2", "L3", "Z21",
+    "T3", "D2", "W0", "J10", "X2", "Z12", "S0", "J03", "J01", "X1", "W0b", "W11", "X3", "Z20", "Z31",
+    "D3", "Rw0", "Rw1", "Z22", "W10", "W2", "F0", "F2", "W3",
 )
 
 
@@ -202,11 +201,11 @@
 
 def kernel(
     tok, grd, ids, slots, counts, score, gpre, upre, wds, wgs, wus, wg, wu, wd,
-    gtok, gscore, gsg, gsd, ggate, gup, gdown, TH,
+    gtok, gscore, gsg, gsd, ggate, gup, gdown, TH, RH,
     G, R, TV, SB, RV, dg_v, du_v, wds_v, wgs_v, wus_v, wg_v, wu_v, wd_v, dguT, hidT, acc_gu, acc_d,
-    rgu, rguT, rhT, BP, BR, MS, BK, WS, W, WH, WF, WX, WD, DH, DF, DX,
+    rgu, rguT, rhT, BP, BR, MS, BK, WS, RS, W, WH, WF, WX, WD, DH, DF, DX,
     XA, ZH, ZF, XB, info, mine, QS, QR,
-    lsem, tsem, wsem, gss, grs, tss, trs, rss, rrs, ass, ars, bss, brs, dss, drs, css, crs,
+    lsem, tsem, wsem, rsem, gss, grs, tss, trs, rss, rrs, ass, ars, bss, brs, dss, drs, css, crs,
     xss, xrs, zss, zrs, wss, wrs, hss, hrs, iss, irs, qss, qrs, credit,
 ):
     p = Place()
@@ -306,28 +305,28 @@
 
         lax.fori_loop(0, width // 512, part, 0)
 
-    slot_of, free = {}, [0, 1]
-
-    def token_load(i):
-        slot_of[i] = free.pop(0)
-        tg.twin(*NEED[i])
-        token_copy(i).start()
-
     def token_copy(i):
         j = p.chip(*CHIP[i])
-        return pltpu.make_async_copy(TH.at[pl.ds(2 * j, 2)], TV.at[slot_of[i]], tsem.at[slot_of[i]])
+        return pltpu.make_async_copy(TH.at[pl.ds(2 * j, 2)], TV.at[i % 2], tsem.at[i % 2])
+
+    def token_load(i):
+        for k in (2 * i, 2 * i + 1):
+            tg.twin(*NEED[k])
+            token_copy(k).start()
 
     def token_unit(i):
-        token_copy(i).wait()
-        j, slot = p.chip(*CHIP[i]), slot_of[i]
-
-        def part(k, carry):
-            cs = cols(k, 512)
-            acc_gu[:, cs] += dot_nn(dguT[j], TV[slot, :, :, cs].reshape(256, 512))
+        token_copy(2 * i).wait()
+        token_copy(2 * i + 1).wait()
+        j, k = p.chip(*CHIP[2 * i]), p.chip(*CHIP[2 * i + 1])
+
+        def part(n, carry):
+            cs = cols(n, 512)
+            acc_gu[:, cs] += dot_nn(dguT[j], TV[0, :, :, cs].reshape(256, 512)) + dot_nn(
+                dguT[k], TV[1, :, :, cs].reshape(256, 512)
+            )
             return carry
 
         lax.fori_loop(0, width // 512, part, 0)
-        free.append(slot)
 
     def r_unit(m):
         if m == 0:
@@ -392,25 +391,35 @@
             pltpu.make_async_copy(WS.at[slot, 2], gdown.at[0, :, cols(k, 256)], wsem.at[slot, 2]),
         )
 
+    def w_load(k, slot):
+        return pltpu.make_async_copy(RH.at[:, :, cols(k, 256)], RS.at[slot], rsem.at[slot])
+
     def w_unit(k, carry):
         slot = k % 2
+        w_load(k, slot).wait()
+
+        @pl.when(k + 1 < width // 256)
+        def _():
+            w_load(k + 1, 1 - slot).start()
 
         @pl.when(k >= 2)
         def _():
             for copy in w_copies(k - 2, slot):
                 copy.wait()
 
-        cs = cols(k, 256)
-        gu = dot_nn(rguT[...], R[:, 0:32, cs].reshape(512, 256))
+        gu = dot_nn(rguT[...], RS[slot, :, 0:32].reshape(512, 256))
         WS[slot, 0] = gu[0:256].T.astype(BF)
         WS[slot, 1] = gu[256:512].T.astype(BF)
-        WS[slot, 2] = dot_nn(rhT[...], R[:, 32:64, cs].reshape(512, 256)).astype(BF)
+        WS[slot, 2] = dot_nn(rhT[...], RS[slot, :, 32:64].reshape(512, 256)).astype(BF)
         for copy in w_copies(k, slot):
             copy.start()
         return carry
 
+    rows_out = pltpu.make_async_copy(R, RH, lsem.at[12])
+
     def r_free():
         rg.finish()
+        rows_out.wait()
         pl.semaphore_signal(credit, inc=1, device_id=p.at(0, 0, True), device_id_type=MESH)
 
     half = (pl.ds(0, 160), pl.ds(160, 160))
@@ -595,7 +604,8 @@
 
     fixed = {
         "Rown": rows_own, "Town": tokens_own, "g2": gg.own_rest, "t2": tg.own_rest, "r2": rg.own_rest, "Rb": r_back, "Rs": r_send, "Rf": r_free,
-        "Rw0": lambda: lax.fori_loop(0, 5, w_unit, 0), "Rw1": lambda: lax.fori_loop(5, 10, w_unit, 0),
+        "Rh": rows_out.start,
+        "Rw0": lambda: (w_load(0, 0).start(), lax.fori_loop(0, 5, w_unit, 0)), "Rw1": lambda: lax.fori_loop(5, 10, w_unit, 0),
         "D0": lambda: (turn(acc_d, WD), sum_first(WD, DH, hss, hrs, 1, 0)),
         "D1": lambda: (sum_second(WD, DH, DF, hss, hrs, 1), sum_second(WD, DH, DF, hss, hrs, 0)),
         "D2": lambda: sum_third(WD, DF, DX, hss, hrs), "D3": down_last,
@@ -660,14 +670,15 @@
     def out(*shape, dtype=BF):
         return jax.ShapeDtypeStruct(shape, dtype)
 
-    gtok, gscore, gsg, gsd, ggate, gup, gdown, _ = pl.pallas_call(
+    gtok, gscore, gsg, gsd, ggate, gup, gdown, _, _ = pl.pallas_call(
         kernel,
         out_shape=(
             out(tok_dev, width), out(1, tok_dev, dtype=F32), out(2, rows, ff), out(rows, ff),
             out(1, width, ff), out(1, width, ff), out(1, ff, width), out(16, tok_dev, width),
+            out(16, 64, width),
         ),
         in_specs=[ANY, ANY, VM, VM, SM, VM] + [ANY] * 8,
-        out_specs=(VM, VM, VM, VM, ANY, ANY, ANY, ANY),
+        out_specs=(VM, VM, VM, VM, ANY, ANY, ANY, ANY, ANY),
         scratch_shapes=[
             vm(16, tok_dev, width), vm(16, 64, width), vm(2, 2, tok_dev, width),
             vm(8, 16, width // 2), vm(8, 16, width // 2),
@@ -676,12 +687,12 @@
             vm(8, 2 * ff, 256), vm(ff, 256), vm(2 * ff, width, dtype=F32), vm(ff, width, dtype=F32),
             vm(512, 2 * ff), vm(2 * ff, 512), vm(ff, 512),
             vm(8, 2, 32, wide), vm(8, 32, wide), vm(8, 32, wide), vm(8, 32, wide),
-            vm(2, 3, 256, 256),
+            vm(2, 3, 256, 256), vm(2, 16, 64, 256),
             vm(2, 8, rows, ff), vm(2, 2, 2, rows // 2, ff), vm(2, 2, 2, rows, ff), vm(2, rows, ff),
             vm(1, 8, rows, ff), vm(2, 2, 1, rows // 2, ff), vm(2, 2, 1, rows, ff), vm(1, rows, ff),
             vm(4, tok_dev, RCUT), vm(3, 2, tok_dev // 2, most), vm(3, 2, tok_dev, most), vm(tok_dev, width - RCUT),
             vm(2, 4, 8, 128, dtype=F32), vm(8, 128, dtype=F32), vm(2, 4, 8, 128, dtype=F32), vm(7, 8, 128, dtype=F32),
-            dma((12,)), dma((2,)), dma((2, 3)),
+            dma((13,)), dma((2,)), dma((2, 3)), dma((2,)),
             dma((N_SLOT,)), dma((N_SLOT,)), dma((N_SLOT,)), dma((N_SLOT,)), dma((N_SLOT,)), dma((N_SLOT,)),
             dma((7,)), dma((7,)), dma((7,)), dma((7,)), dma((1,)), dma((1,)), dma((16,)), dma((16,)),
             dma((5,)), dma((5,)), dma((3, 4)), dma((3, 4)), dma((2, 5)), dma((2, 5)), dma((2, 5)), dma((2, 5)),

time: 150 us -> 148 us (0.987); the launches traced: 150 us -> 146 us
  Pallas kernels: 149 us -> 145 us
    pallas_call x1, Pallas kernels: 146 us -> 141 us  [shards(): pl.pallas_call(kernel, out_shape=(out(tok_dev, width), out(1, tok_dev, dt...]
where the time goes in v3:
time: 148 us; the launch traced here: 146 us
  Pallas kernels  145 us (98%)
    pallas_call x1, Pallas kernels, shards(): pl.pallas_call(kernel, out_shape=(out(tok_dev, width), out(1, tok_dev, dt...  141 us
    pallas_call x1, Pallas kernels, shards(): pl.pallas_call(store_kernel, out_shape=tuple((out(*shape, dtype=dtype) fo...  3.74 us

profile of v3, /device:TPU:6, one launch (start us, length us, event | category | flops | bytes accessed | tf_op | source)
XLA Modules:
  0.0 145.9 jit_solution(10094364760956941646)
XLA Ops:
  0.6 141.4 %shard_map.197 = (bf16[128,2560]{1,0:T(8,128)(2,1)}, f32[1,128]{1,0:T(1,128)}, bf16[2,320,256]{2,1,0:T(8,128)(2,1)}, bf16[320,256]{1,0:T(8,128)(2,1)}, bf16[1,25...) custom-call(bf16[128,2560]{1,0:T(8,128)(2,1)} %tok.1, ...), custom_call_target="tpu_custom_call" | custom-call | tf_op jit(solution)/shard_map/pallas_call | solution.py:673
  142.0 3.7 %shard_map.198 = (bf16[1,2560,256]{2,1,0:T(8,128)(2,1)}, bf16[1,2560,256]{2,1,0:T(8,128)(2,1)}, bf16[1,256,2560]{2,1,0:T(8,128)(2,1)}, bf16[128,2560]{1,0:T(8,12...) custom-call(bf16[128,2560]{1,0:T(8,128)(2,1)} %get-tuple-element.23., ...), custom_call_target="tpu_custom_call" | custom-call | tf_op jit(solution)/shard_map/pallas_call | solution.py:712

commit v4 on v3

--- a/solution.py
+++ b/solution.py
@@ -172,16 +172,16 @@
 CUT = 1152
 RCUT = 1024
 ORDER = (
-    "G0", "g2", "Rown", "r2", "rzA+", "rzA-", "rxB", "M00", "gzA+", "gzB-", "gzA-", "gzB+", "rhA-",
-    "rzB-", "rzB+", "gxA0", "rxA-", "gxB", "rzX-", "rzX+", "rhA+", "G1", "G2", "rxA+", "rxA0", "ghA-",
-    "Town", "t2", "rhB-", "G3", "ghA+", "ghB+", "rhX+", "rxh+", "ghB-", "rxh-", "rhB+", "rhX-", "R0",
-    "R1", "Rb", "Rh", "M03", "G6", "gzX+", "gxA+", "gzX-", "gxA-", "Rs", "tzA-", "tzA+", "gxh-", "Rf",
-    "M02", "M10", "N10", "M01", "tzB+", "N01", "tzB-", "gxh+", "G4", "N00", "ghX+", "N02", "G5", "txB",
-    "N03", "L1", "M11", "ghX-", "txA0", "thA+", "N11", "M13", "N13", "thB-", "T1", "J02", "L0", "thA-",
-    "Z10", "G7", "D0", "M12", "N12", "J11", "S1", "tzX+", "txA+", "tzX-", "J13", "txA-", "T0", "thB+",
-    "J12", "Z11", "S2", "D1", "txh+", "L2", "J00", "txh-", "thX-", "thX+", "S3", "T2", "L3", "Z21",
-    "T3", "D2", "W0", "J10", "X2", "Z12", "S0", "J03", "J01", "X1", "W0b", "W11", "X3", "Z20", "Z31",
-    "D3", "Rw0", "Rw1", "Z22", "W10", "W2", "F0", "F2", "W3",
+    "g2", "Rown", "G0", "r2", "rzA+", "rzA-", "rxB", "M00", "gzB-", "gzA+", "gzA-", "rhA-", "gxA0",
+    "rzB+", "rzB-", "rhA+", "gzB+", "rxA-", "gxB", "rzX+", "rzX-", "rxA+", "rxA0", "rxh-", "G2", "G1",
+    "ghA-", "Town", "ghA+", "t2", "rxh+", "rhX+", "ghB+", "rhX-", "ghB-", "rhB-", "rhB+", "R0", "R1",
+    "Rb", "Rh", "G6", "M03", "G3", "gxA+", "gxh-", "gzX+", "gzX-", "Rs", "Rf", "tzA-", "tzA+", "gxh+",
+    "gxA-", "M02", "M01", "tzB+", "tzB-", "G4", "N02", "N01", "M10", "N00", "G5", "L1", "ghX+", "txA0",
+    "ghX-", "txB", "M11", "N11", "thA+", "thA-", "N03", "M13", "N13", "N10", "T1", "L0", "G7", "J02",
+    "Z10", "D0", "M12", "N12", "J11", "S1", "txA-", "txA+", "tzX-", "tzX+", "T0", "J12", "D1", "Z11",
+    "L2", "thB-", "txh-", "thB+", "txh+", "S2", "thX+", "thX-", "J13", "S3", "J00", "T2", "L3", "Z21",
+    "D2", "T3", "W0", "X2", "J10", "J01", "Z12", "S0", "J03", "X1", "W0b", "W11", "Z20", "Z31", "Rw0",
+    "Rw1", "X3", "Z22", "W10", "D3", "W2", "F2", "F0", "W3",
 )
 
 

time: 148 us -> 147 us (level)
  no operation moved by 1% of the time
where the time goes in v4:
time: 147 us; the launch traced here: 145 us
  Pallas kernels  144 us (98%)
    pallas_call x1, Pallas kernels, shards(): pl.pallas_call(kernel, out_shape=(out(tok_dev, width), out(1, tok_dev, dt...  140 us
    pallas_call x1, Pallas kernels, shards(): pl.pallas_call(store_kernel, out_shape=tuple((out(*shape, dtype=dtype) fo...  3.74 us

profile of v4, /device:TPU:6, one launch (start us, length us, event | category | flops | bytes accessed | tf_op | source)
XLA Modules:
  0.0 144.9 jit_solution(15831707070765635654)
XLA Ops:
  0.6 140.3 %shard_map.197 = (bf16[128,2560]{1,0:T(8,128)(2,1)}, f32[1,128]{1,0:T(1,128)}, bf16[2,320,256]{2,1,0:T(8,128)(2,1)}, bf16[320,256]{1,0:T(8,128)(2,1)}, bf16[1,25...) custom-call(bf16[128,2560]{1,0:T(8,128)(2,1)} %tok.1, ...), custom_call_target="tpu_custom_call" | custom-call | tf_op jit(solution)/shard_map/pallas_call | solution.py:673
  141.0 3.7 %shard_map.198 = (bf16[1,2560,256]{2,1,0:T(8,128)(2,1)}, bf16[1,2560,256]{2,1,0:T(8,128)(2,1)}, bf16[1,256,2560]{2,1,0:T(8,128)(2,1)}, bf16[128,2560]{1,0:T(8,12...) custom-call(bf16[128,2560]{1,0:T(8,128)(2,1)} %get-tuple-element.23., ...), custom_call_target="tpu_custom_call" | custom-call | tf_op jit(solution)/shard_map/pallas_call | solution.py:712

commit v5 on v4

--- a/solution.py
+++ b/solution.py
@@ -172,14 +172,14 @@
 CUT = 1152
 RCUT = 1024
 ORDER = (
-    "g2", "Rown", "G0", "r2", "rzA+", "rzA-", "rxB", "M00", "gzB-", "gzA+", "gzA-", "rhA-", "gxA0",
-    "rzB+", "rzB-", "rhA+", "gzB+", "rxA-", "gxB", "rzX+", "rzX-", "rxA+", "rxA0", "rxh-", "G2", "G1",
-    "ghA-", "Town", "ghA+", "t2", "rxh+", "rhX+", "ghB+", "rhX-", "ghB-", "rhB-", "rhB+", "R0", "R1",
-    "Rb", "Rh", "G6", "M03", "G3", "gxA+", "gxh-", "gzX+", "gzX-", "Rs", "Rf", "tzA-", "tzA+", "gxh+",
-    "gxA-", "M02", "M01", "tzB+", "tzB-", "G4", "N02", "N01", "M10", "N00", "G5", "L1", "ghX+", "txA0",
-    "ghX-", "txB", "M11", "N11", "thA+", "thA-", "N03", "M13", "N13", "N10", "T1", "L0", "G7", "J02",
+    "g2", "Rown", "G0", "r2", "rzA+", "rzA-", "rxB", "M00", "gzB-", "gzA+", "gzA-", "gzB+", "rhA-",
+    "gxA0", "rzB+", "rzB-", "rhA+", "rxA-", "gxB", "rzX+", "rzX-", "G2", "rxA+", "G1", "rxA0", "ghA-",
+    "Town", "ghA+", "t2", "ghB+", "rxh+", "rxh-", "rhX+", "rhX-", "ghB-", "rhB-", "rhB+", "R0", "R1",
+    "Rb", "G6", "M03", "Rh", "G3", "gxA+", "gxh-", "gzX+", "gzX-", "Rs", "Rf", "M01", "tzA-", "gxA-",
+    "tzA+", "gxh+", "M02", "tzB+", "tzB-", "G4", "N02", "N01", "N00", "G5", "L1", "M10", "ghX+", "txA0",
+    "txB", "M11", "ghX-", "N11", "thA+", "N03", "thA-", "M13", "N13", "N10", "T1", "L0", "G7", "J02",
     "Z10", "D0", "M12", "N12", "J11", "S1", "txA-", "txA+", "tzX-", "tzX+", "T0", "J12", "D1", "Z11",
-    "L2", "thB-", "txh-", "thB+", "txh+", "S2", "thX+", "thX-", "J13", "S3", "J00", "T2", "L3", "Z21",
+    "L2", "thB-", "txh-", "thB+", "txh+", "S2", "thX-", "thX+", "J13", "S3", "J00", "T2", "L3", "Z21",
     "D2", "T3", "W0", "X2", "J10", "J01", "Z12", "S0", "J03", "X1", "W0b", "W11", "Z20", "Z31", "Rw0",
     "Rw1", "X3", "Z22", "W10", "D3", "W2", "F2", "F0", "W3",
 )

time: 147 us -> 146 us (level)
  no operation moved by 1% of the time
where the time goes in v5:
time: 146 us; the launch traced here: 145 us
  Pallas kernels  144 us (99%)
    pallas_call x1, Pallas kernels, shards(): pl.pallas_call(kernel, out_shape=(out(tok_dev, width), out(1, tok_dev, dt...  140 us
    pallas_call x1, Pallas kernels, shards(): pl.pallas_call(store_kernel, out_shape=tuple((out(*shape, dtype=dtype) fo...  3.74 us

profile of v5, /device:TPU:6, one launch (start us, length us, event | category | flops | bytes accessed | tf_op | source)
XLA Modules:
  0.0 144.9 jit_solution(15729998210111820583)
XLA Ops:
  0.6 140.4 %shard_map.197 = (bf16[128,2560]{1,0:T(8,128)(2,1)}, f32[1,128]{1,0:T(1,128)}, bf16[2,320,256]{2,1,0:T(8,128)(2,1)}, bf16[320,256]{1,0:T(8,128)(2,1)}, bf16[1,25...) custom-call(bf16[128,2560]{1,0:T(8,128)(2,1)} %tok.1, ...), custom_call_target="tpu_custom_call" | custom-call | tf_op jit(solution)/shard_map/pallas_call | solution.py:673
  141.0 3.7 %shard_map.198 = (bf16[1,2560,256]{2,1,0:T(8,128)(2,1)}, bf16[1,2560,256]{2,1,0:T(8,128)(2,1)}, bf16[1,256,2560]{2,1,0:T(8,128)(2,1)}, bf16[128,2560]{1,0:T(8,12...) custom-call(bf16[128,2560]{1,0:T(8,128)(2,1)} %get-tuple-element.23., ...), custom_call_target="tpu_custom_call" | custom-call | tf_op jit(solution)/shard_map/pallas_call | solution.py:712
